TPU v7x, 256 devices: a whole 4x4x8 slice. The times are simulated.
256 devices in a mesh: ctx: 32 (over z, y_hi, core), head: 8 (over y_lo, x).
Axes of the slice: x: 4, y: 4 (y_hi: 2, y_lo: 2; y = y_hi * 2 + y_lo), z: 8, core: 2. Of those that a mesh axis runs over, the one named last changes fastest.
Arguments:
- tokens: bfloat16 [8192, 2048], P('ctx'), may hold values from -6 to 6
- w_qkv: bfloat16 [2048, 3, 2048], P(None, None, 'head'), may hold values from -0.125 to 0.125
- w_out: bfloat16 [2048, 2048], P('head'), may hold values from -0.125 to 0.125
- grad_out: bfloat16 [8192, 2048], P('ctx'), may hold values from -6 to 6
Outputs:
- grad_x: bfloat16 [8192, 2048], P('ctx', 'head')
- grad_wqkv: float32 [2048, 3, 2048], P('ctx', None, 'head')
- grad_wout: float32 [2048, 2048], P('head', 'ctx')
All inputs are finite; a program needn't handle non-finite values.
Results may differ from a plain program's by a relative error of at most 0.023.
Values may be sent and summed in bfloat16 or wider, within the bound.
No kernel may reach another device: no remote copies, remote signals or barrier semaphores. Data moves between devices by JAX's collectives and lax.ppermute only.
A program may use at most 128 MiB of HBM per device.

v0:
```python
import functools

import jax
import jax.numpy as jnp
import numpy as np
from jax import lax
from jax.experimental import pallas as pl
from jax.experimental.pallas import tpu as pltpu
from jax.sharding import PartitionSpec as P

DH = 128
BLK = 16
T = 256
ROWS = 256
NEAR = 2 * BLK
REM = 64
FAR = 96
SCALE = DH**-0.5
BF = jnp.bfloat16
F32 = jnp.float32

STARTS = {1: 0, 2: 128, 3: 192, 4: 224, 5: 240, 6: 248, 7: 252}


def tables():
    spread = np.zeros((T, ROWS), np.float32)
    mean = np.zeros((ROWS, T), np.float32)
    pairs = np.zeros((ROWS, ROWS), np.float32)
    for level, start in STARTS.items():
        factor = 2**level
        for row in range(T // factor):
            spread[row * factor : (row + 1) * factor, start + row] = 1.0
            mean[start + row, row * factor : (row + 1) * factor] = 1.0 / factor
        if level <= 3:
            for block in range(T // factor // BLK):
                other = start + (block ^ 1) * BLK
                mine = start + block * BLK
                pairs[mine : mine + BLK, other : other + BLK] = 1.0
    block_of = np.arange(T) // BLK
    band = (np.abs(block_of[:, None] - block_of[None, :]) <= 1).astype(np.float32)
    rim = np.zeros((T, REM), np.float32)
    rim[:BLK, :BLK] = np.eye(BLK)
    rim[T - BLK :, BLK:NEAR] = np.eye(BLK)
    rim[:, NEAR:] = spread[:, 224:]
    rim_mean = rim.copy()
    rim_mean[:, NEAR:] = mean.T[:, 224:]
    meets = np.zeros((REM, FAR), np.float32)
    meets[0:16, 0:16] = 1.0
    meets[16:32, 16:32] = 1.0
    meets[32:48, 32:48] = 1.0
    meets[48:56, 48:64] = 1.0
    meets[56:60, 64:80] = 1.0
    meets[60:62, 80:96] = 1.0
    bf = lambda array: np.asarray(array, dtype=BF)
    return {
        "spread": bf(spread),
        "gather": bf(spread.T),
        "mean": bf(mean),
        "unmean": bf(mean.T),
        "band": band,
        "pairs": pairs,
        "rim": bf(rim),
        "rim_mean": bf(rim_mean),
        "meets": meets,
        "met": np.ascontiguousarray(meets.T),
    }


def dot(left, right):
    return jnp.dot(left, right, preferred_element_type=F32)


def dot_nt(left, right):
    return lax.dot_general(left, right, (((1,), (1,)), ((), ())), preferred_element_type=F32)


def dot_tn(left, right):
    return lax.dot_general(left, right, (((0,), (0,)), ((), ())), preferred_element_type=F32)


def dot_two(exact, right):
    high = right.astype(BF)
    low = (right - high.astype(F32)).astype(BF)
    return dot(exact, high) + dot(exact, low)


def normed(values):
    scale = lax.rsqrt(jnp.mean(values * values, axis=-1, keepdims=True) + 1e-06)
    return values * scale, scale


def norm_back(unit, scale, grad):
    return scale * (grad - unit * jnp.mean(grad * unit, axis=-1, keepdims=True))


def head(array, number):
    return array[:, number * DH : (number + 1) * DH]


def pack_den(d_den_0, d_den_1):
    lane = lax.broadcasted_iota(jnp.int32, (T, DH), 1)
    total = jnp.zeros((T, DH), F32)
    for number, array in enumerate((d_den_0, d_den_1)):
        high = array.astype(BF).astype(F32)
        total = jnp.where(lane == 2 * number, high, total)
        total = jnp.where(lane == 2 * number + 1, array - high, total)
    return total.astype(BF)


def packed_den(sums, number):
    at = 2 * DH + 2 * number
    return sums[:, at : at + 1] + sums[:, at + 1 : at + 2]


def with_ones(values):
    return jnp.concatenate([values, jnp.ones_like(values)], axis=1)


class Calls:
    def __init__(self):
        self.token = None

    def __call__(self, kernel, outs, *args, placed=False, after=(), flops=1e10):
        first = tuple(after) if self.token is None else (self.token,) + tuple(after)
        skipped = len(first)
        args = first + args
        specs = [pl.BlockSpec(memory_space=pltpu.VMEM)] * len(args)

        def body(*refs):
            refs = refs[skipped:-1]
            if placed:
                kernel((lax.axis_index("ctx"), lax.axis_index("head")), *refs)
            else:
                kernel(*refs)

        shapes = [jax.ShapeDtypeStruct(shape, dtype) for shape, dtype in outs]
        shapes.append(jax.ShapeDtypeStruct((8, 128), F32))
        results = pl.pallas_call(
            body,
            out_shape=tuple(shapes),
            in_specs=specs,
            out_specs=tuple(pl.BlockSpec(memory_space=pltpu.VMEM) for _ in shapes),
            compiler_params=pltpu.CompilerParams(vmem_limit_bytes=44 * 1024 * 1024),
            cost_estimate=pl.CostEstimate(
                flops=int(flops), bytes_accessed=1000, transcendentals=0
            ),
        )(*args)
        self.token = results[-1]
        return results[:-1]


def packed(rows):
    half = rows.shape[1] // 2
    return jnp.concatenate([rows[:, :half], rows[:, half:]], axis=0)


def unpacked(rows):
    half = rows.shape[0] // 2
    return jnp.concatenate([rows[:half], rows[half:]], axis=1)


def edges_kernel(pos, tokens, near_out, far_out, level_5_out):
    even = pos[0] % 2 == 0
    row = lax.broadcasted_iota(jnp.int32, (BLK, T), 0)
    col = lax.broadcasted_iota(jnp.int32, (BLK, T), 1)
    mean = dot(jnp.where(col // BLK == row, 1.0 / BLK, 0.0).astype(BF), tokens[...])
    row = lax.broadcasted_iota(jnp.int32, (8, T), 0)
    col = lax.broadcasted_iota(jnp.int32, (8, T), 1)
    wide = dot(jnp.where(col // NEAR == row, 1.0 / NEAR, 0.0).astype(BF), tokens[...])
    first = tokens[:BLK].astype(F32)
    last = tokens[T - BLK :].astype(F32)
    near_out[:BLK] = mean.astype(BF)
    near_out[BLK:] = jnp.where(even, last, first).astype(BF)
    far_out[...] = jnp.where(even, first, last).astype(BF)
    level_5_out[...] = packed(wide).astype(BF)


def project_kernel(tokens, weights, mean, qkv_out, coarse_out):
    tok = tokens[...]
    parts = [dot(tok, weights[number]).astype(BF) for number in range(3)]
    qkv = jnp.concatenate(parts, axis=1)
    qkv_out[...] = qkv
    coarse_out[...] = dot(mean[...], qkv)


def half_of_rows(whole, number):
    width = whole.shape[0] // 32
    return jnp.concatenate(
        [whole[(2 * j + number) * width : (2 * j + number + 1) * width] for j in range(16)], axis=0
    )


def d_attn_kernel(pos, grad_out, w_out, tokens, d_attn_out, own_out, other_out):
    d_attn_out[...] = dot_nt(grad_out[...], w_out[...]).astype(BF)
    even = pos[0] % 2 == 0
    for number, array in enumerate((tokens, grad_out)):
        cols = slice(number * T, (number + 1) * T)
        turned = array[...].T
        halves = half_of_rows(turned, 0), half_of_rows(turned, 1)
        own_out[:, cols] = jnp.where(even, halves[0], halves[1])
        other_out[:, cols] = jnp.where(even, halves[1], halves[0])


def merged(factor, first, second):
    row = lax.broadcasted_iota(jnp.int32, (BLK, BLK), 0)
    col = lax.broadcasted_iota(jnp.int32, (BLK, BLK), 1)
    same = row // 8 == col // 8
    source = col % 8 // 2
    left = jnp.where(jnp.logical_and(same, source == row % 8), factor, 0.0).astype(BF)
    right = jnp.where(jnp.logical_and(same, source + 4 == row % 8), factor, 0.0).astype(BF)
    return (dot(left, first) + dot(right, second)).astype(BF)


def merge_kernel(factor, first, second, *rest):
    if len(rest) > 1:
        rest[1][...] = rest[0][...]
    rest[-1][...] = merged(factor, first[...], second[...])


def bundle_kernel(level_5, level_6, third, fourth, chained, near, out):
    out[:BLK] = level_5[...]
    out[BLK : 2 * BLK] = level_6[...]
    out[2 * BLK : 3 * BLK] = merged(0.5, third[...], fourth[...])
    out[3 * BLK : 5 * BLK] = packed(chained[...].astype(F32)).astype(BF)
    out[5 * BLK :] = packed(near[...].astype(F32)).astype(BF)


EDGE = 2 * BLK
LEVEL_5 = 3 * BLK
SECOND = 3 * BLK


def grads_5_kernel(level_4, own, side, out):
    out[:BLK] = level_4[...]
    out[BLK : BLK + SECOND] = own[...]
    out[BLK + SECOND :] = side[...]


def grads_6(pos, own, other):
    row = lax.broadcasted_iota(jnp.int32, (8, BLK), 0)
    col = lax.broadcasted_iota(jnp.int32, (8, BLK), 1)
    pairs = jnp.where(col // 2 == row, 1.0, 0.0).astype(BF)
    low, high = by_side(pos, own, other)
    blocks = []
    for rows in (low, high):
        both = [rows[at : at + 8] for at in (LEVEL_5, LEVEL_5 + SECOND)]
        blocks.append(dot(pairs, jnp.concatenate(both, axis=0).astype(BF)))
    y_low = pos[0] // 2 % 2 == 0
    edges = []
    for rows, mine in ((high, jnp.logical_not(y_low)), (low, y_low)):
        here, there = rows[EDGE : EDGE + BLK], rows[EDGE + SECOND : EDGE + SECOND + BLK]
        edges.append(jnp.where(mine, here, there))
    return jnp.concatenate(blocks, axis=0), edges


def grads_7_kernel(pos, own, other, level_6, up, down, level_6_out, level_7_out, far_out):
    z_even = pos[0] // 4 % 2 == 0
    from_up, from_down = up[-BLK:].astype(F32), down[-BLK:].astype(F32)
    half = from_up.shape[1] // 2
    came_6 = jnp.where(z_even, from_down[:, :half], from_up[:, :half]).astype(BF)
    level_6_out[...] = came_6
    level_7_out[...] = merged(1.0, level_6[...], came_6)
    low, high = by_side(pos, own[...].astype(F32), other[...].astype(F32))
    at = slice(EDGE + SECOND, EDGE + SECOND + BLK)
    y_low = pos[0] // 2 % 2 == 0
    left = jnp.where(y_low, from_up[:, half:], high[at])
    right = jnp.where(y_low, low[at], from_down[:, half:])
    far_out[...] = jnp.where(pos[0] % 2 == 0, left, right).astype(BF)


def local_units(qkv, coarse, number):
    query = head(qkv, number).astype(F32)
    key = head(qkv, 2 + number).astype(F32)
    return (
        normed(query),
        normed(key),
        head(qkv, 4 + number),
        normed(head(coarse, number)),
        normed(head(coarse, 2 + number)),
        head(coarse, 4 + number).astype(BF),
    )


def local_weights(units, band, pairs):
    (qn, _), (kn, _), _, (qc, _), (kc, _), _ = units
    near = jnp.exp(dot_nt(qn.astype(BF), kn.astype(BF)) * SCALE) * band
    far = jnp.exp(dot_nt(qc.astype(BF), kc.astype(BF)) * SCALE) * pairs
    return near, far


def local_forward_kernel(
    qkv_ref, coarse_ref, band, pairs, spread, out, probs, turned, units_out, scales_out
):
    qkv = qkv_ref[...]
    coarse = coarse_ref[...]
    for number in range(2):
        units = local_units(qkv, coarse, number)
        near, far = (array.astype(BF) for array in local_weights(units, band[...], pairs[...]))
        total = dot(near, with_ones(units[2]))
        part = dot(far, with_ones(units[5]))
        out[:, number * 2 * DH : (number + 1) * 2 * DH] = total + dot_two(spread[...], part)
        probs[:, number * T : (number + 1) * T] = near
        probs[:, (2 + number) * T : (3 + number) * T] = far
        swapped = (units[1], units[0], units[2], units[4], units[3], units[5])
        near, far = (array.astype(BF) for array in local_weights(swapped, band[...], pairs[...]))
        turned[:, number * T : (number + 1) * T] = near
        turned[:, (2 + number) * T : (3 + number) * T] = far
        for place, (unit, scale) in enumerate((units[0], units[1], units[3], units[4])):
            at = slice((2 * place + number) * DH, (2 * place + number + 1) * DH)
            units_out[:, at] = unit
            scales_out[:, at] = jnp.broadcast_to(scale, (T, DH))


def by_side(pos, ours, others):
    even = pos[0] % 2 == 0
    return jnp.where(even, ours, others), jnp.where(even, others, ours)


def remote_rows(pos, arrived, far, levels):
    left, right = by_side(pos, far, arrived[BLK:])
    return jnp.concatenate([left, right, arrived[:BLK]] + levels, axis=0)


def own_rows(fine, coarse):
    return jnp.concatenate([fine[:BLK], fine[T - BLK :], coarse[224:]], axis=0)


def exists(pos, shape, axis):
    where = lax.broadcasted_iota(jnp.int32, shape, axis)
    no_left = jnp.logical_and(pos[0] == 0, where < BLK)
    no_right = jnp.logical_and(pos[0] == 31, jnp.logical_and(where >= BLK, where < NEAR))
    return jnp.where(jnp.logical_or(no_left, no_right), 0.0, 1.0)


def remote_weights(pos, query, remote, meets, number):
    key, key_scale = normed(head(remote, number))
    value = head(remote, 2 + number).astype(BF)
    weights = jnp.exp(dot_nt(query, key.astype(BF)) * SCALE) * meets * exists(pos, (REM, FAR), 1)
    return weights, key, key_scale, value


def gathered_rows(pos, far, mine_ref, theirs_ref):
    mine = mine_ref[...].astype(F32)
    theirs = theirs_ref[...].astype(F32)
    levels = []
    for level in range(3):
        at = slice(level * BLK, (level + 1) * BLK)
        levels += by_side(pos, unpacked(mine[at]), unpacked(theirs[at]))
    arrived = unpacked(theirs[5 * BLK :])
    return remote_rows(pos, arrived, far[...].astype(F32), levels), theirs


def turn_far_kernel(
    pos, weights_ref, near, far, mine_ref, theirs_ref, own_out, other_out, query_out
):
    even = pos[0] % 2 == 0
    rows, theirs = gathered_rows(pos, far, mine_ref, theirs_ref)
    known = near[...].astype(F32)
    left, right = by_side(pos, known[BLK:], unpacked(theirs[3 * BLK : 5 * BLK]))
    other = jnp.concatenate([left, right, known[:BLK], rows[3 * BLK :]], axis=0)
    for array, out in ((rows, own_out), (other, other_out)):
        turned = array.T
        out[...] = jnp.where(even, half_of_rows(turned, 0), half_of_rows(turned, 1)).astype(BF)
    query_out[...] = dot(rows.astype(BF), weights_ref[0]).astype(BF)


def remote_forward_kernel(
    pos, weights_ref, qkv_ref, coarse_ref, local_ref, d_attn, far, mine_ref, theirs_ref,
    meets, rim, gather,
    attn_out, both_out, level_4_out, share_out, remote_out,
):
    rows, _ = gathered_rows(pos, far, mine_ref, theirs_ref)
    even = pos[0] % 2 == 0
    rows = rows.astype(BF)
    remote = jnp.concatenate([dot(rows, weights_ref[part]) for part in (1, 2)], axis=1)
    remote = remote.astype(BF)
    remote_out[...] = remote
    remote = remote.astype(F32)
    d_nums, d_dens = [], []
    for number in range(2):
        fine = qkv_ref[:, number * DH : (number + 1) * DH].astype(F32)
        query = normed(own_rows(fine, coarse_ref[:, number * DH : (number + 1) * DH]))[0]
        weights, _, _, value = remote_weights(
            pos, query.astype(BF), remote, meets[...], number
        )
        part = dot(weights.astype(BF), with_ones(value)).astype(BF)
        total = local_ref[:, number * 2 * DH : (number + 1) * 2 * DH] + dot(rim[...], part)
        cols = slice(number * DH, (number + 1) * DH)
        inverse = 1.0 / total[:, DH:]
        attn = total[:, :DH] * inverse
        attn_out[:, cols] = attn.astype(BF)
        d_num = (d_attn[:, cols].astype(F32) * inverse).astype(BF)
        d_den = -jnp.sum(d_num.astype(F32) * attn, axis=-1, keepdims=True)
        d_nums.append(d_num)
        d_dens.append(jnp.broadcast_to(d_den, (T, DH)))
    both = jnp.concatenate(d_nums + [pack_den(*d_dens)], axis=1)
    both_out[...] = both
    sums = dot(gather[224:256, :], both)
    for number in range(2):
        den_sums = jnp.broadcast_to(packed_den(sums, number), (NEAR, DH))
        for offset, full, row_sums in (
            (0, d_nums[number].astype(F32), head(sums, number)),
            (2 * DH, d_dens[number], den_sums),
        ):
            at = slice(offset + number * DH, offset + (number + 1) * DH)
            first = full[:BLK]
            last = full[T - BLK :]
            level_4_out[:, at] = row_sums[:BLK].astype(BF)
            share = [
                jnp.where(even, last, first),
                jnp.where(even, first, last),
                row_sums[BLK:],
            ]
            share_out[:, at] = jnp.concatenate(share, axis=0).astype(BF)


def local_backward_kernel(
    pos, qkv_ref, coarse_ref, probs, turned, units_ref, scales_ref, attn_ref, both_ref,
    remote_ref, meets, gather, unmean,
    y_out, dkv_out,
):
    remote = remote_ref[...].astype(F32)
    both = both_ref[...]
    y_out[:T, T:] = attn_ref[...]
    sums = dot(gather[...], both)
    dens = both[:, 2 * DH :]
    dens_c = pack_den(*(jnp.broadcast_to(packed_den(sums, number), (T, DH)) for number in (0, 1)))
    lane = lax.broadcasted_iota(jnp.int32, (T, DH), 1)
    dqns, dkns, dvns, tables = [], [], [], []
    for number in range(2):
        cols = slice(number * DH, (number + 1) * DH)
        vals = slice((2 + number) * DH, (3 + number) * DH)
        qn, kn, qc, kc = (head(units_ref, 2 * place + number) for place in range(4))
        qc_scale, kc_scale = (head(scales_ref, 2 * place + number) for place in (2, 3))
        picks = jnp.where(lane // 2 == number, 1.0, 0.0).astype(BF)
        sides = []
        for place, d_num, den, value, query, key in (
            (0, head(both, number), dens, head(qkv_ref, 4 + number), qn, kn),
            (2, head(sums, number).astype(BF), dens_c,
             head(coarse_ref, 4 + number).astype(BF), qc, kc),
        ):
            at = slice((place + number) * T, (place + number + 1) * T)
            grad = jnp.concatenate([d_num, den], axis=1)
            value = jnp.concatenate([value, picks], axis=1)
            weights, weights_t = probs[:, at], turned[:, at]
            d_score = (weights * dot_nt(grad, value) * SCALE).astype(BF)
            d_score_t = (weights_t * dot_nt(value, grad) * SCALE).astype(BF)
            sides.append(
                (
                    dot(d_score, key.astype(BF)),
                    dot(d_score_t, query.astype(BF)),
                    dot(weights_t, d_num),
                )
            )
        (dqn, dkn, dvn), (dqc, dkc, dvc) = sides
        query = own_rows(qn, qc).astype(BF)
        weights, key_r, key_scale, value_r = remote_weights(
            pos, query, remote, meets[...], number
        )
        d_num_r = own_rows(head(both, number).astype(F32), head(sums, number)).astype(BF)
        den_r = own_rows(dens.astype(F32), dens_c.astype(F32)).astype(BF)
        picks = picks[:FAR]
        d_rem = dot_nt(
            jnp.concatenate([d_num_r, den_r], axis=1), jnp.concatenate([value_r, picks], axis=1)
        )
        d_rem = (weights * d_rem * SCALE).astype(BF)
        y_out[2 * T : 2 * T + FAR, cols] = norm_back(
            key_r, key_scale, dot_tn(d_rem, query)
        ).astype(BF)
        y_out[2 * T : 2 * T + FAR, vals] = dot_tn(weights.astype(BF), d_num_r).astype(BF)
        dqr = dot(d_rem, key_r.astype(BF))
        dqns.append(
            jnp.concatenate(
                [dqn[:BLK] + dqr[:BLK], dqn[BLK : T - BLK], dqn[T - BLK :] + dqr[BLK:NEAR]], axis=0
            )
        )
        dqc = jnp.concatenate([dqc[:224], dqc[224:] + dqr[NEAR:]], axis=0)
        dkns.append(dkn)
        dvns.append(dvn)
        tables += [norm_back(qc, qc_scale, dqc), norm_back(kc, kc_scale, dkc), dvc]
    table = dot(unmean[...], jnp.concatenate(tables, axis=1).astype(BF))
    for number in range(2):
        cols = slice(number * DH, (number + 1) * DH)
        vals = slice((2 + number) * DH, (3 + number) * DH)
        qn, kn = (head(units_ref, 2 * place + number) for place in (0, 1))
        q_scale, k_scale = (head(scales_ref, 2 * place + number) for place in (0, 1))
        dq, dk, dv = (head(table, 3 * number + place) for place in range(3))
        y_out[:T, cols] = (norm_back(qn, q_scale, dqns[number]) + dq).astype(BF)
        dk = norm_back(kn, k_scale, dkns[number]) + dk
        dv = dvns[number] + dv
        dkv_out[:, cols] = dk
        dkv_out[:, vals] = dv
        y_out[T : 2 * T, cols] = dk.astype(BF)
        y_out[T : 2 * T, vals] = dv.astype(BF)


def remote_backward_kernel(
    pos, qkv_ref, coarse_ref, local_ref, remote_ref, own_ref, other_ref, g_far, g_6, g_7,
    met, rim_mean, dkv_out,
):
    other = other_ref[...].astype(F32)
    at = slice(LEVEL_5 + SECOND, LEVEL_5 + SECOND + 8)
    sides = by_side(pos, own_ref[...].astype(F32)[at], other[at])
    levels = list(sides) + [g_6[...].astype(F32), g_7[...].astype(F32)]
    grads = remote_rows(pos, other[:NEAR], g_far[...].astype(F32), levels)
    for number in range(2):
        query = normed(head(remote_ref, number).astype(F32))[0].astype(BF)
        k_cols = slice((2 + number) * DH, (3 + number) * DH)
        v_cols = slice((4 + number) * DH, (5 + number) * DH)
        key, key_scale = normed(
            own_rows(qkv_ref[:, k_cols].astype(F32), coarse_ref[:, k_cols])
        )
        vals = own_rows(qkv_ref[:, v_cols].astype(F32), coarse_ref[:, v_cols]).astype(BF)
        weights = jnp.exp(dot_nt(query, key.astype(BF)) * SCALE)
        weights = weights * met[...] * exists(pos, (FAR, REM), 0)
        d_num = head(grads, number).astype(BF)
        d_den = head(grads, 2 + number)[:, :1]
        d_score = (weights * (dot_nt(d_num, vals) + d_den) * SCALE).astype(BF)
        dk = norm_back(key, key_scale, dot_tn(d_score, query))
        dv = dot_tn(weights.astype(BF), d_num)
        more = dot_two(rim_mean[...], jnp.concatenate([dk, dv], axis=1))
        k_cols = slice(number * DH, (number + 1) * DH)
        v_cols = slice((2 + number) * DH, (3 + number) * DH)
        dkv_out[:, k_cols] = (local_ref[:, k_cols] + more[:, :DH]).astype(BF)
        dkv_out[:, v_cols] = (local_ref[:, v_cols] + more[:, DH:]).astype(BF)


def weight_part(pos, step, own_half, other_half, own, other, own_far, other_far, out):
    z = pos[0] // 4
    width = own_half.shape[0] // 8
    at = pl.ds(pl.multiple_of((z + step) % 8 * width, width), width)
    for cols in (slice(0, T), slice(T, 2 * T)):
        total = dot(own_half[at, cols], own[:T, cols])
        total += dot(other_half[at, cols], other[:T, cols])
        out[:width, cols] = total.astype(BF)
    total = dot(own_half[at, :T], own[T : 2 * T]) + dot(own_far[at, :], own[2 * T :])
    total += dot(other_half[at, :T], other[T : 2 * T])
    total += dot(other_far[at, :], other[2 * T :])
    out[:width, 2 * T :] = total.astype(BF)


def first_weight_kernel(pos, g_own, g_other, *refs):
    up, down, level_6_out = refs[-3:]
    weight_part(pos, 4, *refs[:-3], up)
    weight_part(pos, 5, *refs[:-3], down)
    level_6, edges = grads_6(pos, g_own[...].astype(F32), g_other[...].astype(F32))
    level_6_out[...] = level_6.astype(BF)
    rows = up.shape[0] - BLK
    for out, edge in zip((up, down), edges):
        out[rows:] = jnp.concatenate([level_6, edge], axis=1).astype(BF)


def weight_kernel(steps, pos, *refs):
    for step, out in zip(steps, refs[-len(steps) :]):
        weight_part(pos, step, *refs[: -len(steps)], out)


def own_weight_kernel(pos, *refs):
    keep_0, keep_1, send, total = refs[-4:]
    half = total.shape[0] // 2
    low = pos[0] // 2 % 2 == 0
    for step, keep in enumerate((keep_0, keep_1)):
        weight_part(pos, step, *refs[:-4], total)
        first, second = total[:half].astype(F32), total[half:].astype(F32)
        keep[...] = jnp.where(low, first, second).astype(BF)
        send[step * half : (step + 1) * half] = jnp.where(low, second, first).astype(BF)


def add_kernel(up, part_up, down, part_down, up_out, down_out):
    rows = part_up.shape[0]
    up_out[...] = (up[:rows].astype(F32) + part_up[...].astype(F32)).astype(BF)
    down_out[...] = (down[:rows].astype(F32) + part_down[...].astype(F32)).astype(BF)


def by_row_half(pos, total, straight, cross):
    low = pos[0] // 2 % 2 == 0
    half = total.shape[0] // 2
    straight[...] = jnp.where(low, total[:half], total[half:]).astype(BF)
    cross[...] = jnp.where(low, total[half:], total[:half]).astype(BF)


def third_step_kernel(pos, up, part_up, down, part_down, *outs):
    by_row_half(pos, up[...].astype(F32) + part_up[...].astype(F32), *outs[:2])
    by_row_half(pos, down[...].astype(F32) + part_down[...].astype(F32), *outs[2:])


def last_step_kernel(cross, straight, keep, side, out):
    total = cross[...].astype(F32) + straight[...].astype(F32)
    rows = total.shape[0]
    out[...] = (total + keep[...].astype(F32) + side[rows:].astype(F32)).astype(BF)


def finish_kernel(*refs):
    w_qkv, w_out = refs[-2:]
    total = refs[0][...].astype(F32)
    for ref in refs[1:-2]:
        total += ref[: total.shape[0]].astype(F32)
    w_qkv[0] = total[:, :T]
    w_qkv[1] = total[:, 2 * T : 3 * T]
    w_qkv[2] = total[:, 3 * T :]
    w_out[...] = total[:, T : 2 * T]


def grad_x_kernel(pos, y, dkv, weights, *outs):
    x = pos[1] % 4
    side = pos[1] // 4
    for step in range(4):
        for turn in range(2):
            target = (side + turn) % 2 * 4 + (x + step) % 4
            rows = pl.ds(pl.multiple_of(target * T, T), T)
            total = dot_nt(y[:T, :T], weights[0, rows, :])
            total += dot_nt(dkv[:, :T], weights[1, rows, :])
            total += dot_nt(dkv[:, T:], weights[2, rows, :])
            outs[step][turn * T : (turn + 1) * T] = total.astype(BF)


def sum_x_kernel(first, second, third, fourth, keep, send):
    total = first[...].astype(F32) + second[...].astype(F32)
    total = total + third[...].astype(F32) + fourth[...].astype(F32)
    keep[...] = total[:T]
    send[...] = total[T:].astype(BF)


def last_x_kernel(keep, came, out):
    out[...] = (keep[...] + came[...].astype(F32)).astype(BF)


def local(tokens, w_qkv, w_out, grad_out):
    const = {name: jnp.asarray(array) for name, array in tables().items()}
    head_count = lax.axis_size("head")
    weights = jnp.transpose(w_qkv, (1, 0, 2))
    width = tokens.shape[1]
    wide = 3 * T

    def swap(array, bit):
        return lax.ppermute(array, "ctx", [(i, i ^ bit) for i in range(32)])

    def chain(array):
        pairs = [(i, (i + 1) % 32) for i in range(1, 32, 2)]
        return lax.ppermute(array, "ctx", pairs + [(b, a) for a, b in pairs])

    def turn_z(array, step, side=0):
        return lax.ppermute(
            array, "ctx", [(i, (i // 4 + step) % 8 * 4 + (i % 4 ^ side)) for i in range(32)]
        )

    call = Calls()

    near, far, level_5 = call(
        edges_kernel, [((NEAR, width), BF), ((BLK, width), BF), ((BLK, width // 2), BF)],
        tokens, placed=True,
    )
    side = swap(level_5, 2)
    qkv, coarse = call(
        project_kernel, [((T, wide), BF), ((ROWS, wide), F32)], tokens, weights, const["mean"]
    )
    far, level_6 = call(
        functools.partial(merge_kernel, 0.5), [((BLK, width), BF), ((BLK, width // 2), BF)],
        level_5, side, far, flops=1e3)
    sixes = [swap(level_6, bit) for bit in (4, 8, 12)]
    chained = chain(far)
    forward, probs, turned, units, scales = call(
        local_forward_kernel,
        [((T, 2 * T), F32)] + [((T, 4 * T), BF)] * 2 + [((T, 4 * T), F32)] * 2,
        qkv, coarse, const["band"], const["pairs"], const["spread"],
    )
    (mine,) = call(
        bundle_kernel, [((9 * BLK, width // 2), BF)], side, *sixes, chained, near, flops=1e3)
    theirs = swap(mine, 1)
    d_attn, own_half, other_half = call(
        d_attn_kernel,
        [((T, T), BF), ((width // 2, 2 * T), BF), ((width // 2, 2 * T), BF)],
        grad_out, w_out, tokens, placed=True,
    )
    sent_half = swap(other_half, 1)
    attn, both, g_4, g_share, remote = call(
        remote_forward_kernel,
        [
            ((T, T), BF), ((T, 3 * DH), BF), ((BLK, 2 * T), BF), ((3 * BLK, 2 * T), BF),
            ((FAR, 2 * T), BF),
        ],
        weights, qkv, coarse, forward, d_attn, chained, mine, theirs,
        const["meets"], const["rim"], const["gather"], placed=True,
    )
    g_side = swap(g_share, 2)
    y, dkv_local = call(
        local_backward_kernel, [((2 * T + FAR, 2 * T), BF), ((T, 2 * T), F32)],
        qkv, coarse, probs, turned, units, scales, attn, both, remote,
        const["meets"], const["gather"], const["unmean"], placed=True,
    )
    other_y = swap(y, 1)
    (g_own,) = call(
        grads_5_kernel, [((7 * BLK, 2 * T), BF)], g_4, g_share, g_side, flops=1e3
    )
    g_other = swap(g_own, 1)
    own_far, other_far, remote_q = call(
        turn_far_kernel, [((width // 2, FAR), BF)] * 2 + [((FAR, T), BF)],
        weights, near, chained, mine, theirs, placed=True,
    )
    chunk = width // 16
    factors = (own_half, sent_half, y, other_y, own_far, other_far)
    whole, half = ((chunk, 4 * T), BF), ((chunk // 2, 4 * T), BF)
    small = ((BLK, 2 * T), BF)
    message = ((chunk + BLK, 4 * T), BF)
    up, down, g_6 = call(
        first_weight_kernel, [message, message, small], g_own, g_other, *factors, placed=True
    )
    up, down = turn_z(up, 1), turn_z(down, -1)
    keep, keep_1, send, _ = call(
        own_weight_kernel, [half, half, whole, whole], *factors, placed=True
    )
    from_side = swap(send, 2)
    steps = (3, 6, 2, 7)
    products = call(
        functools.partial(weight_kernel, steps), [whole] * 4, *factors, placed=True
    )
    parts = dict(zip(steps, products))
    came_6, g_7, g_far = call(
        grads_7_kernel, [small] * 3, g_own, g_other, g_6, up, down, placed=True, flops=1e3
    )
    came_7 = swap(g_7, 8)
    up, down = call(
        add_kernel, [whole] * 2, up, parts[3], down, parts[6], after=[from_side], flops=1e3
    )
    up, down = turn_z(up, 1), turn_z(down, -1)
    (dkv,) = call(
        remote_backward_kernel, [((T, 2 * T), BF)],
        qkv, coarse, dkv_local, remote_q, g_own, g_other, g_far, came_6, came_7,
        const["met"], const["rim_mean"], placed=True,
    )
    if head_count == 8:
        pieces = call(grad_x_kernel, [((2 * T, T), BF)] * 4, y, dkv, weights, placed=True)

        def turn_x(array, step):
            pairs = [(i, i // 4 * 4 + (i % 4 + step) % 4) for i in range(8)]
            return lax.ppermute(array, "head", pairs)

        came = [turn_x(pieces[step], step) for step in (1, 2, 3)]
    up_straight, up_cross, straight, cross = call(
        third_step_kernel, [half] * 4, up, parts[2], down, parts[7], placed=True, flops=1e3
    )
    up = [turn_z(up_cross, 1, 2), turn_z(up_straight, 1)]
    from_down = [turn_z(straight, -1), turn_z(cross, -1, 2)]
    if head_count == 8:
        keep_x, send_x = call(
            sum_x_kernel, [((T, T), F32), ((T, T), BF)], pieces[0], *came, flops=1e3
        )
        came_x = lax.ppermute(send_x, "head", [(i, i ^ 4) for i in range(8)])
    (last,) = call(last_step_kernel, [half], *up, keep_1, from_side, flops=1e3)
    from_up = [turn_z(last, 1)]
    grad_wqkv, grad_wout = call(
        finish_kernel, [((3, chunk // 2, T), F32), ((chunk // 2, T), F32)],
        keep, from_side, *from_down, *from_up,
    )
    if head_count == 8:
        (grad_x,) = call(last_x_kernel, [((T, T), BF)], keep_x, came_x)
    else:
        flat = jnp.transpose(weights, (1, 0, 2)).reshape(width, wide)
        grad_x = dot_nt(jnp.concatenate([y[:T, :T], dkv], axis=1), flat).astype(BF)
    return grad_x, jnp.transpose(grad_wqkv, (1, 0, 2)), grad_wout.T


def solution(mesh):
    placed = (P("ctx", None), P(None, None, "head"), P("head", None), P("ctx", None))
    return jax.shard_map(
        local,
        mesh=mesh,
        in_specs=placed,
        out_specs=(P("ctx", "head"), P("ctx", None, "head"), P("head", "ctx")),
        check_vma=False,
    )
```

profile of v0, /device:TPU:2, one launch (start us, length us, event | category | flops | bytes accessed | tf_op | source)
XLA Modules:
  0.0 75.2 jit_solution(1907545336596009167)
XLA Ops:
  0.7 1.4 %copy-done.1 = bf16[256,2048]{1,0:T(8,128)(2,1)S(1)} copy-done((bf16[256,2048]{1,0:T(8,128)(2,1)S(1)}, bf16[256,2048]{1,0:T(8,128)(2,1)}, u32[]{:S(2)}) %copy-start.1) | copy-done | bytes 1048600
  2.4 3.2 %collective-permute-start = (bf16[16,1024]{1,0:T(8,128)(2,1)S(1)}, bf16[16,1024]{1,0:T(8,128)(2,1)S(1)}, u32[]{:S(2)}, u32[]{:S(2)}) collective-permute-start(bf16[16,1024]{1,0:T(8,128)(2,1)S(1)} %get-tuple-element.83.refs_1_), channel_id=1, source_target_pairs={{0,16},{8,24},{16,0},{24,8},{32,48},{40,56},{48,32},{56,40},{64,80... | collective-permute-start | bytes 98312 | tf_op jit(solution)/shard_map/ppermute | solution.py:636
  5.7 1.3 %shard_map.158 = (bf16[256,768]{1,0:T(8,128)(2,1)S(1)}, f32[256,768]{1,0:T(8,128)S(1)}, f32[8,128]{1,0:T(8,128)S(1)}) custom-call(f32[8,128]{1,0:T(8,128)S(1)} %get-tuple-element.81.refs_0_, bf16[256,2048]{1,0:T(8,128)(2,1)S(1)} %copy-done.1, bf16[3,2048,256]{2,1,0:T(8,128)(2,1)S(1)} %bitcast.3, bf16[256,256]{1,0:T(8,128)(2,1)S(1)} %copy-done.10), custom_call_target="tpu_custom_call" | custom-call | flops 10000000000 | bytes 1000 | tf_op jit(solution)/shard_map/pallas_call | solution.py:138
  7.0 0.9 %collective-permute-done.refs_2_.refs_1_ = bf16[16,1024]{1,0:T(8,128)(2,1)S(1)} collective-permute-done((bf16[16,1024]{1,0:T(8,128)(2,1)S(1)}, bf16[16,1024]{1,0:T(8,128)(2,1)S(1)}, u32[]{:S(2)}, u32[]{:S(2)}) %collective-permute-start) | collective-permute-done | bytes 32800 | tf_op jit(solution)/shard_map/ppermute | solution.py:636
  8.0 4.6 %collective-permute-start.3 = (bf16[16,1024]{1,0:T(8,128)(2,1)S(1)}, bf16[16,1024]{1,0:T(8,128)(2,1)S(1)}, u32[]{:S(2)}, u32[]{:S(2)}) collective-permute-start(bf16[16,1024]{1,0:T(8,128)(2,1)S(1)} %get-tuple-element.89), channel_id=1, source_target_pairs={{0,96},{8,104},{16,112},{24,120},{32,64},{40,72},{48,80},{56,88},{... | collective-permute-start | bytes 98312 | tf_op jit(solution)/shard_map/ppermute | solution.py:636
  13.3 5.1 %collective-permute-start.4 = (bf16[16,2048]{1,0:T(8,128)(2,1)S(1)}, bf16[16,2048]{1,0:T(8,128)(2,1)S(1)}, u32[]{:S(2)}, u32[]{:S(2)}) collective-permute-start(bf16[16,2048]{1,0:T(8,128)(2,1)S(1)} %get-tuple-element.90), channel_id=1, source_target_pairs={{8,16},{24,32},{40,48},{56,64},{72,80},{88,96},{104,112},{120,128}... | collective-permute-start | bytes 196616 | tf_op jit(solution)/shard_map/ppermute | solution.py:640
  18.4 1.3 %shard_map.160 = (f32[256,512]{1,0:T(8,128)S(1)}, bf16[256,1024]{1,0:T(8,128)(2,1)S(1)}, bf16[256,1024]{1,0:T(8,128)(2,1)S(1)}, f32[256,1024]{1,0:T(8,128)S(1)},...) custom-call(f32[8,128]{1,0:T(8,128)S(1)} %get-tuple-element.85.refs_0_, ...), custom_call_target="tpu_custom_call" | custom-call | flops 10000000000 | bytes 1000 | tf_op jit(solution)/shard_map/pallas_call | solution.py:138
  22.3 1.5 %shard_map.163 = (bf16[256,256]{1,0:T(8,128)(2,1)S(1)}, bf16[256,384]{1,0:T(8,128)(2,1)S(1)}, bf16[16,512]{1,0:T(8,128)(2,1)S(1)}, bf16[48,512]{1,0:T(8,128)(2,1...) custom-call(f32[8,128]{1,0:T(8,128)S(1)} %get-tuple-element.93.refs_0_, bf16[3,2048,256]{2,1,0:T(8,128)(2,1)S(1)} %bitcast.4, ...), custom_call_target="tpu_custom_call" | custom-call | flops 10000000000 | bytes 1000 | tf_op jit(solution)/shard_map/pallas_call | solution.py:138
  23.8 1.3 %collective-permute-start.6 = (bf16[48,512]{1,0:T(8,128)(2,1)S(1)}, bf16[48,512]{1,0:T(8,128)(2,1)S(1)}, u32[]{:S(2)}, u32[]{:S(2)}) collective-permute-start(bf16[48,512]{1,0:T(8,128)(2,1)S(1)} %get-tuple-element.107.refs_2_), channel_id=1, source_target_pairs={{0,16},{8,24},{16,0},{24,8},{32,48},{40,56},{48,32},{56,40},{64,80... | collective-permute-start | bytes 147464 | tf_op jit(solution)/shard_map/ppermute | solution.py:636
  25.1 2.1 %shard_map.164 = (bf16[608,512]{1,0:T(8,128)(2,1)S(1)}, f32[256,512]{1,0:T(8,128)S(1)}, f32[8,128]{1,0:T(8,128)S(1)}) custom-call(f32[8,128]{1,0:T(8,128)S(1)} %get-tuple-element.97.refs_0_, bf16[256,768]{1,0:T(8,128)(2,1)S(1)} %get-tuple-element.86.refs_1_.refs_2_, f32[256,768]{1,0:T(8,128)S(1)} %get-tuple-element.87.refs_2_.refs_3_, ...), custom_call_target="tpu_custom_call" | custom-call | flops 10000000000 | bytes 1000 | tf_op jit(solution)/shard_map/pallas_call | solution.py:138
  27.3 2.2 %collective-permute-done.6.refs_3_ = bf16[48,512]{1,0:T(8,128)(2,1)S(1)} collective-permute-done((bf16[48,512]{1,0:T(8,128)(2,1)S(1)}, bf16[48,512]{1,0:T(8,128)(2,1)S(1)}, u32[]{:S(2)}, u32[]{:S(2)}) %collective-permute-start.6) | collective-permute-done | bytes 49184 | tf_op jit(solution)/shard_map/ppermute | solution.py:636
  30.2 0.9 %collective-permute-done.7.refs_2_.refs_6_ = bf16[112,512]{1,0:T(8,128)(2,1)S(1)} collective-permute-done((bf16[112,512]{1,0:T(8,128)(2,1)S(1)}, bf16[112,512]{1,0:T(8,128)(2,1)S(1)}, u32[]{:S(2)}, u32[]{:S(2)}) %collective-permute-start.7) | collective-permute-done | bytes 114720 | tf_op jit(solution)/shard_map/ppermute | solution.py:636
  32.0 3.8 %collective-permute-start.11 = (bf16[144,1024]{1,0:T(8,128)(2,1)S(1)}, bf16[144,1024]{1,0:T(8,128)(2,1)S(1)}, u32[]{:S(2)}, u32[]{:S(2)}) collective-permute-start(bf16[144,1024]{1,0:T(8,128)(2,1)S(1)} %get-tuple-element.121), channel_id=1, source_target_pairs={{0,224},{8,232},{16,240},{24,248},{32,0},{40,8},{48,16},{56,24},{6... | collective-permute-start | bytes 884744 | tf_op jit(solution)/shard_map/ppermute | solution.py:643
  35.8 1.3 %shard_map.168 = (bf16[64,1024]{1,0:T(8,128)(2,1)S(1)}, bf16[64,1024]{1,0:T(8,128)(2,1)S(1)}, bf16[128,1024]{1,0:T(8,128)(2,1)S(1)}, bf16[128,1024]{1,0:T(8,128)(2,1)}, f32[8,128]{1,0:T(8,128)S(1)}) custom-call(f32[8,128]{1,0:T(8,128)S(1)} %get-tuple-element.116.refs_0_, bf16[1024,512]{1,0:T(8,128)(2,1)S(1)} %get-tuple-element.111.refs_3_.refs_1_, ...), custom_call_target="tpu_custom_call" | custom-call | flops 10000000000 | bytes 1000 | tf_op jit(solution)/shard_map/pallas_call | solution.py:138
  37.1 2.8 %collective-permute-start.12 = (bf16[128,1024]{1,0:T(8,128)(2,1)S(1)}, bf16[128,1024]{1,0:T(8,128)(2,1)S(1)}, u32[]{:S(2)}, u32[]{:S(2)}) collective-permute-start(bf16[128,1024]{1,0:T(8,128)(2,1)S(1)} %get-tuple-element.123), channel_id=1, source_target_pairs={{0,16},{8,24},{16,0},{24,8},{32,48},{40,56},{48,32},{56,40},{64,80... | collective-permute-start | bytes 786440 | tf_op jit(solution)/shard_map/ppermute | solution.py:636
  39.9 1.0 %shard_map.169 = (bf16[128,1024]{1,0:T(8,128)(2,1)S(1)}, bf16[128,1024]{1,0:T(8,128)(2,1)S(1)}, bf16[128,1024]{1,0:T(8,128)(2,1)S(1)}, bf16[128,1024]{1,0:T(8,128)(2,1)S(1)}, f32[8,128]{1,0:T(8,128)S(1)}) custom-call(f32[8,128]{1,0:T(8,128)S(1)} %get-tuple-element.117.refs_0_, bf16[1024,512]{1,0:T(8,128)(2,1)S(1)} %get-tuple-element.111.refs_3_.refs_1_, ...), custom_call_target="tpu_custom_call" | custom-call | flops 10000000000 | bytes 1000 | tf_op jit(solution)/shard_map/pallas_call | solution.py:138
  40.9 2.1 %collective-permute-done.10.refs_4_.refs_2_ = bf16[144,1024]{1,0:T(8,128)(2,1)S(1)} collective-permute-done((bf16[144,1024]{1,0:T(8,128)(2,1)S(1)}, bf16[144,1024]{1,0:T(8,128)(2,1)S(1)}, u32[]{:S(2)}, u32[]{:S(2)}) %collective-permute-start.10) | collective-permute-done | bytes 294944 | tf_op jit(solution)/shard_map/ppermute | solution.py:643
  43.1 3.2 %collective-permute-start.13 = (bf16[16,512]{1,0:T(8,128)(2,1)S(1)}, bf16[16,512]{1,0:T(8,128)(2,1)S(1)}, u32[]{:S(2)}, u32[]{:S(2)}) collective-permute-start(bf16[16,512]{1,0:T(8,128)(2,1)S(1)} %get-tuple-element.131), channel_id=1, source_target_pairs={{0,64},{8,72},{16,80},{24,88},{32,96},{40,104},{48,112},{56,120},{... | collective-permute-start | bytes 49160 | tf_op jit(solution)/shard_map/ppermute | solution.py:636
  46.8 2.8 %collective-permute-start.14 = (bf16[128,1024]{1,0:T(8,128)(2,1)S(1)}, bf16[128,1024]{1,0:T(8,128)(2,1)S(1)}, u32[]{:S(2)}, u32[]{:S(2)}) collective-permute-start(bf16[128,1024]{1,0:T(8,128)(2,1)S(1)} %get-tuple-element.135), channel_id=1, source_target_pairs={{0,32},{8,40},{16,48},{24,56},{32,64},{40,72},{48,80},{56,88},{64,... | collective-permute-start | bytes 786440 | tf_op jit(solution)/shard_map/ppermute | solution.py:643
  50.1 1.0 %shard_map.172 = (bf16[256,512]{1,0:T(8,128)(2,1)S(1)}, f32[8,128]{1,0:T(8,128)S(1)}) custom-call(f32[8,128]{1,0:T(8,128)S(1)} %get-tuple-element.126.refs_0_, bf16[256,768]{1,0:T(8,128)(2,1)S(1)} %get-tuple-element.86.refs_1_.refs_2_, f32[256,768]{1,0:T(8,128)S(1)} %get-tuple-element.87.refs_2_.refs_3_, f32[256,512]{1,0:T(8,128)S(1)} %get-tuple-element.127.refs_3_, ...), custom_call_target="tpu_custom_call" | custom-call | flops 10000000000 | bytes 1000 | tf_op jit(solution)/shard_map/pallas_call | solution.py:138
  51.1 1.0 %shard_map.173 = (bf16[512,256]{1,0:T(8,128)(2,1)S(1)}, bf16[512,256]{1,0:T(8,128)(2,1)S(1)}, bf16[512,256]{1,0:T(8,128)(2,1)S(1)}, bf16[512,256]{1,0:T(8,128)(2,1)S(1)}, f32[8,128]{1,0:T(8,128)S(1)}) custom-call(f32[8,128]{1,0:T(8,128)S(1)} %get-tuple-element.132.refs_0_, bf16[608,512]{1,0:T(8,128)(2,1)S(1)} %get-tuple-element.113.refs_5_.refs_3_.refs_1_, ...), custom_call_target="tpu_custom_call" | custom-call | flops 10000000000 | bytes 1000 | tf_op jit(solution)/shard_map/pallas_call | solution.py:138
  52.1 1.6 %collective-permute-start.16 = (bf16[512,256]{1,0:T(8,128)(2,1)S(1)}, bf16[512,256]{1,0:T(8,128)(2,1)S(1)}, u32[]{:S(2)}, u32[]{:S(2)}) collective-permute-start(bf16[512,256]{1,0:T(8,128)(2,1)S(1)} %get-tuple-element.141), channel_id=1, source_target_pairs={{0,1},{1,2},{2,3},{3,0},{4,5},{5,6},{6,7},{7,4},{8,9},{9,10},{10,1... | collective-permute-start | bytes 786440 | tf_op jit(solution)/shard_map/ppermute | solution.py:736
  53.7 1.1 %collective-permute-start.17 = (bf16[512,256]{1,0:T(8,128)(2,1)S(1)}, bf16[512,256]{1,0:T(8,128)(2,1)S(1)}, u32[]{:S(2)}, u32[]{:S(2)}) collective-permute-start(bf16[512,256]{1,0:T(8,128)(2,1)S(1)} %get-tuple-element.142), channel_id=1, source_target_pairs={{0,2},{1,3},{2,0},{3,1},{4,6},{5,7},{6,4},{7,5},{8,10},{9,11},{10,... | collective-permute-start | bytes 786440 | tf_op jit(solution)/shard_map/ppermute | solution.py:736
  54.8 2.2 %collective-permute-start.18 = (bf16[512,256]{1,0:T(8,128)(2,1)S(1)}, bf16[512,256]{1,0:T(8,128)(2,1)S(1)}, u32[]{:S(2)}, u32[]{:S(2)}) collective-permute-start(bf16[512,256]{1,0:T(8,128)(2,1)S(1)} %get-tuple-element.143), channel_id=1, source_target_pairs={{0,3},{1,0},{2,1},{3,2},{4,7},{5,4},{6,5},{7,6},{8,11},{9,8},{10,9... | collective-permute-start | bytes 786440 | tf_op jit(solution)/shard_map/ppermute | solution.py:736
  57.1 2.1 %collective-permute-start.19 = (bf16[64,1024]{1,0:T(8,128)(2,1)S(1)}, bf16[64,1024]{1,0:T(8,128)(2,1)S(1)}, u32[]{:S(2)}, u32[]{:S(2)}) collective-permute-start(bf16[64,1024]{1,0:T(8,128)(2,1)S(1)} %get-tuple-element.145), channel_id=1, source_target_pairs={{0,48},{8,56},{16,32},{24,40},{32,80},{40,88},{48,64},{56,72},{64,... | collective-permute-start | bytes 393224 | tf_op jit(solution)/shard_map/ppermute | solution.py:643
  59.4 2.0 %collective-permute-done.16.refs_2_ = bf16[512,256]{1,0:T(8,128)(2,1)S(1)} collective-permute-done((bf16[512,256]{1,0:T(8,128)(2,1)S(1)}, bf16[512,256]{1,0:T(8,128)(2,1)S(1)}, u32[]{:S(2)}, u32[]{:S(2)}) %collective-permute-start.16) | collective-permute-done | bytes 262176 | tf_op jit(solution)/shard_map/ppermute | solution.py:736
  61.4 1.3 %collective-permute-start.21 = (bf16[64,1024]{1,0:T(8,128)(2,1)S(1)}, bf16[64,1024]{1,0:T(8,128)(2,1)S(1)}, u32[]{:S(2)}, u32[]{:S(2)}) collective-permute-start(bf16[64,1024]{1,0:T(8,128)(2,1)S(1)} %get-tuple-element.150), channel_id=1, source_target_pairs={{0,224},{8,232},{16,240},{24,248},{32,0},{40,8},{48,16},{56,24},{6... | collective-permute-start | bytes 393224 | tf_op jit(solution)/shard_map/ppermute | solution.py:643
  62.7 1.7 %collective-permute-done.17.refs_3_ = bf16[512,256]{1,0:T(8,128)(2,1)S(1)} collective-permute-done((bf16[512,256]{1,0:T(8,128)(2,1)S(1)}, bf16[512,256]{1,0:T(8,128)(2,1)S(1)}, u32[]{:S(2)}, u32[]{:S(2)}) %collective-permute-start.17) | collective-permute-done | bytes 262176 | tf_op jit(solution)/shard_map/ppermute | solution.py:736
  64.4 2.9 %collective-permute-start.22 = (bf16[64,1024]{1,0:T(8,128)(2,1)S(1)}, bf16[64,1024]{1,0:T(8,128)(2,1)S(1)}, u32[]{:S(2)}, u32[]{:S(2)}) collective-permute-start(bf16[64,1024]{1,0:T(8,128)(2,1)S(1)} %get-tuple-element.151), channel_id=1, source_target_pairs={{0,240},{8,248},{16,224},{24,232},{32,16},{40,24},{48,0},{56,8},{6... | collective-permute-start | bytes 393224 | tf_op jit(solution)/shard_map/ppermute | solution.py:643
  67.5 1.5 %collective-permute-start.23 = (bf16[64,1024]{1,0:T(8,128)(2,1)S(1)}, bf16[64,1024]{1,0:T(8,128)(2,1)S(1)}, u32[]{:S(2)}, u32[]{:S(2)}) collective-permute-start(bf16[64,1024]{1,0:T(8,128)(2,1)S(1)} %get-tuple-element.152), channel_id=1, source_target_pairs={{0,32},{8,40},{16,48},{24,56},{32,64},{40,72},{48,80},{56,88},{64,... | collective-permute-start | bytes 393224 | tf_op jit(solution)/shard_map/ppermute | solution.py:643
  69.7 2.2 %collective-permute-done.22.refs_4_ = bf16[64,1024]{1,0:T(8,128)(2,1)S(1)} collective-permute-done((bf16[64,1024]{1,0:T(8,128)(2,1)S(1)}, bf16[64,1024]{1,0:T(8,128)(2,1)S(1)}, u32[]{:S(2)}, u32[]{:S(2)}) %collective-permute-start.22) | collective-permute-done | bytes 131104 | tf_op jit(solution)/shard_map/ppermute | solution.py:643
  71.9 1.9 %collective-permute-done.23.refs_5_ = bf16[64,1024]{1,0:T(8,128)(2,1)S(1)} collective-permute-done((bf16[64,1024]{1,0:T(8,128)(2,1)S(1)}, bf16[64,1024]{1,0:T(8,128)(2,1)S(1)}, u32[]{:S(2)}, u32[]{:S(2)}) %collective-permute-start.23) | collective-permute-done | bytes 131104 | tf_op jit(solution)/shard_map/ppermute | solution.py:643
  (70 shorter events, 9.2 us)
Async XLA Ops:
  0.6 5.0 %copy-start = (bf16[2048,3,256]{2,0,1:T(8,128)(2,1)S(1)}, bf16[2048,3,256]{2,0,1:T(8,128)(2,1)}, u32[]{:S(2)}) copy-start(bf16[2048,3,256]{2,0,1:T(8,128)(2,1)} %param.15) | copy-start | bytes 9437188
  2.0 3.6 %copy-start.10 = (bf16[256,256]{1,0:T(8,128)(2,1)S(1)}, bf16[256,256]{1,0:T(8,128)(2,1)}, u32[]{:S(2)}) copy-start(bf16[256,256]{1,0:T(8,128)(2,1)} %constant.22.clone.refs_3_) | copy-start | bytes 393220
  2.4 5.5 %collective-permute-start = (bf16[16,1024]{1,0:T(8,128)(2,1)S(1)}, bf16[16,1024]{1,0:T(8,128)(2,1)S(1)}, u32[]{:S(2)}, u32[]{:S(2)}) collective-permute-start(bf16[16,1024]{1,0:T(8,128)(2,1)S(1)} %get-tuple-element.83.refs_1_), channel_id=1, source_target_pairs={{0,16},{8,24},{16,0},{24,8},{32,48},{40,56},{48,32},{56,40},{64,80... | collective-permute-start | bytes 98312 | tf_op jit(solution)/shard_map/ppermute | solution.py:636
  5.6 12.7 %copy-start.5 = (f32[256,256]{1,0:T(8,128)S(1)}, f32[256,256]{1,0:T(8,128)}, u32[]{:S(2)}) copy-start(f32[256,256]{1,0:T(8,128)} %constant.25.clone.refs_4_) | copy-start | bytes 786436
  5.6 12.7 %copy-start.6 = (f32[256,256]{1,0:T(8,128)S(1)}, f32[256,256]{1,0:T(8,128)}, u32[]{:S(2)}) copy-start(f32[256,256]{1,0:T(8,128)} %constant.24.clone.refs_3_) | copy-start | bytes 786436
  5.6 12.7 %copy-start.9 = (bf16[256,256]{1,0:T(8,128)(2,1)S(1)}, bf16[256,256]{1,0:T(8,128)(2,1)}, u32[]{:S(2)}) copy-start(bf16[256,256]{1,0:T(8,128)(2,1)} %constant.20.clone.refs_5_) | copy-start | bytes 393220
  8.0 11.7 %collective-permute-start.3 = (bf16[16,1024]{1,0:T(8,128)(2,1)S(1)}, bf16[16,1024]{1,0:T(8,128)(2,1)S(1)}, u32[]{:S(2)}, u32[]{:S(2)}) collective-permute-start(bf16[16,1024]{1,0:T(8,128)(2,1)S(1)} %get-tuple-element.89), channel_id=1, source_target_pairs={{0,96},{8,104},{16,112},{24,120},{32,64},{40,72},{48,80},{56,88},{... | collective-permute-start | bytes 98312 | tf_op jit(solution)/shard_map/ppermute | solution.py:636
  12.6 7.1 %collective-permute-start.2 = (bf16[16,1024]{1,0:T(8,128)(2,1)S(1)}, bf16[16,1024]{1,0:T(8,128)(2,1)S(1)}, u32[]{:S(2)}, u32[]{:S(2)}) collective-permute-start(bf16[16,1024]{1,0:T(8,128)(2,1)S(1)} %get-tuple-element.89), channel_id=1, source_target_pairs={{0,64},{8,72},{16,80},{24,88},{32,96},{40,104},{48,112},{56,120},{... | collective-permute-start | bytes 98312 | tf_op jit(solution)/shard_map/ppermute | solution.py:636
  12.6 7.1 %collective-permute-start.1 = (bf16[16,1024]{1,0:T(8,128)(2,1)S(1)}, bf16[16,1024]{1,0:T(8,128)(2,1)S(1)}, u32[]{:S(2)}, u32[]{:S(2)}) collective-permute-start(bf16[16,1024]{1,0:T(8,128)(2,1)S(1)} %get-tuple-element.89), channel_id=1, source_target_pairs={{0,32},{8,40},{16,48},{24,56},{32,0},{40,8},{48,16},{56,24},{64,96... | collective-permute-start | bytes 98312 | tf_op jit(solution)/shard_map/ppermute | solution.py:636
  13.3 7.3 %collective-permute-start.4 = (bf16[16,2048]{1,0:T(8,128)(2,1)S(1)}, bf16[16,2048]{1,0:T(8,128)(2,1)S(1)}, u32[]{:S(2)}, u32[]{:S(2)}) collective-permute-start(bf16[16,2048]{1,0:T(8,128)(2,1)S(1)} %get-tuple-element.90), channel_id=1, source_target_pairs={{8,16},{24,32},{40,48},{56,64},{72,80},{88,96},{104,112},{120,128}... | collective-permute-start | bytes 196616 | tf_op jit(solution)/shard_map/ppermute | solution.py:640
  20.7 1.6 %collective-permute-start.5 = (bf16[144,1024]{1,0:T(8,128)(2,1)S(1)}, bf16[144,1024]{1,0:T(8,128)(2,1)S(1)}, u32[]{:S(2)}, u32[]{:S(2)}) collective-permute-start(bf16[144,1024]{1,0:T(8,128)(2,1)S(1)} %get-tuple-element.96.refs_7_.refs_4_), channel_id=1, source_target_pairs={{0,8},{8,0},{16,24},{24,16},{32,40},{40,32},{48,56},{56,48},{64,72... | collective-permute-start | bytes 884744 | tf_op jit(solution)/shard_map/ppermute | solution.py:636
  21.4 9.6 %collective-permute-start.8 = (bf16[1024,512]{1,0:T(8,128)(2,1)S(1)}, bf16[1024,512]{1,0:T(8,128)(2,1)S(1)}, u32[]{:S(2)}, u32[]{:S(2)}) collective-permute-start(bf16[1024,512]{1,0:T(8,128)(2,1)S(1)} %get-tuple-element.112), channel_id=1, source_target_pairs={{0,8},{8,0},{16,24},{24,16},{32,40},{40,32},{48,56},{56,48},{64,72... | collective-permute-start | bytes 3145736 | tf_op jit(solution)/shard_map/ppermute | solution.py:636
  23.8 5.6 %collective-permute-start.6 = (bf16[48,512]{1,0:T(8,128)(2,1)S(1)}, bf16[48,512]{1,0:T(8,128)(2,1)S(1)}, u32[]{:S(2)}, u32[]{:S(2)}) collective-permute-start(bf16[48,512]{1,0:T(8,128)(2,1)S(1)} %get-tuple-element.107.refs_2_), channel_id=1, source_target_pairs={{0,16},{8,24},{16,0},{24,8},{32,48},{40,56},{48,32},{56,40},{64,80... | collective-permute-start | bytes 147464 | tf_op jit(solution)/shard_map/ppermute | solution.py:636
  27.2 3.9 %collective-permute-start.9 = (bf16[608,512]{1,0:T(8,128)(2,1)S(1)}, bf16[608,512]{1,0:T(8,128)(2,1)S(1)}, u32[]{:S(2)}, u32[]{:S(2)}) collective-permute-start(bf16[608,512]{1,0:T(8,128)(2,1)S(1)} %get-tuple-element.113.refs_5_.refs_3_.refs_1_), channel_id=1, source_target_pairs={{0,8},{8,0},{16,24},{24,16},{32,40},{40,32},{48,56},{56,48},{64,72... | collective-permute-start | bytes 1867784 | tf_op jit(solution)/shard_map/ppermute | solution.py:636
  29.5 1.6 %collective-permute-start.7 = (bf16[112,512]{1,0:T(8,128)(2,1)S(1)}, bf16[112,512]{1,0:T(8,128)(2,1)S(1)}, u32[]{:S(2)}, u32[]{:S(2)}) collective-permute-start(bf16[112,512]{1,0:T(8,128)(2,1)S(1)} %get-tuple-element.110.refs_1_.refs_5_), channel_id=1, source_target_pairs={{0,8},{8,0},{16,24},{24,16},{32,40},{40,32},{48,56},{56,48},{64,72... | collective-permute-start | bytes 344072 | tf_op jit(solution)/shard_map/ppermute | solution.py:636
  31.7 11.3 %collective-permute-start.10 = (bf16[144,1024]{1,0:T(8,128)(2,1)S(1)}, bf16[144,1024]{1,0:T(8,128)(2,1)S(1)}, u32[]{:S(2)}, u32[]{:S(2)}) collective-permute-start(bf16[144,1024]{1,0:T(8,128)(2,1)S(1)} %get-tuple-element.120), channel_id=1, source_target_pairs={{0,32},{8,40},{16,48},{24,56},{32,64},{40,72},{48,80},{56,88},{64,... | collective-permute-start | bytes 884744 | tf_op jit(solution)/shard_map/ppermute | solution.py:643
  32.0 11.0 %collective-permute-start.11 = (bf16[144,1024]{1,0:T(8,128)(2,1)S(1)}, bf16[144,1024]{1,0:T(8,128)(2,1)S(1)}, u32[]{:S(2)}, u32[]{:S(2)}) collective-permute-start(bf16[144,1024]{1,0:T(8,128)(2,1)S(1)} %get-tuple-element.121), channel_id=1, source_target_pairs={{0,224},{8,232},{16,240},{24,248},{32,0},{40,8},{48,16},{56,24},{6... | collective-permute-start | bytes 884744 | tf_op jit(solution)/shard_map/ppermute | solution.py:643
  37.1 9.6 %collective-permute-start.12 = (bf16[128,1024]{1,0:T(8,128)(2,1)S(1)}, bf16[128,1024]{1,0:T(8,128)(2,1)S(1)}, u32[]{:S(2)}, u32[]{:S(2)}) collective-permute-start(bf16[128,1024]{1,0:T(8,128)(2,1)S(1)} %get-tuple-element.123), channel_id=1, source_target_pairs={{0,16},{8,24},{16,0},{24,8},{32,48},{40,56},{48,32},{56,40},{64,80... | collective-permute-start | bytes 786440 | tf_op jit(solution)/shard_map/ppermute | solution.py:636
  39.9 10.2 %copy-start.11 = (bf16[256,64]{1,0:T(8,128)(2,1)S(1)}, bf16[256,64]{1,0:T(8,128)(2,1)}, u32[]{:S(2)}) copy-start(bf16[256,64]{1,0:T(8,128)(2,1)} %constant.27.clone.refs_11_) | copy-start | bytes 98308
  39.9 10.2 %copy-start.13 = (f32[96,64]{1,0:T(8,128)S(1)}, f32[96,64]{1,0:T(8,128)}, u32[]{:S(2)}) copy-start(f32[96,64]{1,0:T(8,128)} %constant.29.clone.refs_10_) | copy-start | bytes 73732
  43.1 6.9 %collective-permute-start.13 = (bf16[16,512]{1,0:T(8,128)(2,1)S(1)}, bf16[16,512]{1,0:T(8,128)(2,1)S(1)}, u32[]{:S(2)}, u32[]{:S(2)}) collective-permute-start(bf16[16,512]{1,0:T(8,128)(2,1)S(1)} %get-tuple-element.131), channel_id=1, source_target_pairs={{0,64},{8,72},{16,80},{24,88},{32,96},{40,104},{48,112},{56,120},{... | collective-permute-start | bytes 49160 | tf_op jit(solution)/shard_map/ppermute | solution.py:636
  46.8 10.2 %collective-permute-start.14 = (bf16[128,1024]{1,0:T(8,128)(2,1)S(1)}, bf16[128,1024]{1,0:T(8,128)(2,1)S(1)}, u32[]{:S(2)}, u32[]{:S(2)}) collective-permute-start(bf16[128,1024]{1,0:T(8,128)(2,1)S(1)} %get-tuple-element.135), channel_id=1, source_target_pairs={{0,32},{8,40},{16,48},{24,56},{32,64},{40,72},{48,80},{56,88},{64,... | collective-permute-start | bytes 786440 | tf_op jit(solution)/shard_map/ppermute | solution.py:643
  49.5 7.4 %collective-permute-start.15 = (bf16[128,1024]{1,0:T(8,128)(2,1)S(1)}, bf16[128,1024]{1,0:T(8,128)(2,1)S(1)}, u32[]{:S(2)}, u32[]{:S(2)}) collective-permute-start(bf16[128,1024]{1,0:T(8,128)(2,1)S(1)} %get-tuple-element.137), channel_id=1, source_target_pairs={{0,224},{8,232},{16,240},{24,248},{32,0},{40,8},{48,16},{56,24},{6... | collective-permute-start | bytes 786440 | tf_op jit(solution)/shard_map/ppermute | solution.py:643
  52.1 9.3 %collective-permute-start.16 = (bf16[512,256]{1,0:T(8,128)(2,1)S(1)}, bf16[512,256]{1,0:T(8,128)(2,1)S(1)}, u32[]{:S(2)}, u32[]{:S(2)}) collective-permute-start(bf16[512,256]{1,0:T(8,128)(2,1)S(1)} %get-tuple-element.141), channel_id=1, source_target_pairs={{0,1},{1,2},{2,3},{3,0},{4,5},{5,6},{6,7},{7,4},{8,9},{9,10},{10,1... | collective-permute-start | bytes 786440 | tf_op jit(solution)/shard_map/ppermute | solution.py:736
  53.7 10.7 %collective-permute-start.17 = (bf16[512,256]{1,0:T(8,128)(2,1)S(1)}, bf16[512,256]{1,0:T(8,128)(2,1)S(1)}, u32[]{:S(2)}, u32[]{:S(2)}) collective-permute-start(bf16[512,256]{1,0:T(8,128)(2,1)S(1)} %get-tuple-element.142), channel_id=1, source_target_pairs={{0,2},{1,3},{2,0},{3,1},{4,6},{5,7},{6,4},{7,5},{8,10},{9,11},{10,... | collective-permute-start | bytes 786440 | tf_op jit(solution)/shard_map/ppermute | solution.py:736
  54.8 12.5 %collective-permute-start.18 = (bf16[512,256]{1,0:T(8,128)(2,1)S(1)}, bf16[512,256]{1,0:T(8,128)(2,1)S(1)}, u32[]{:S(2)}, u32[]{:S(2)}) collective-permute-start(bf16[512,256]{1,0:T(8,128)(2,1)S(1)} %get-tuple-element.143), channel_id=1, source_target_pairs={{0,3},{1,0},{2,1},{3,2},{4,7},{5,4},{6,5},{7,6},{8,11},{9,8},{10,9... | collective-permute-start | bytes 786440 | tf_op jit(solution)/shard_map/ppermute | solution.py:736
  57.1 10.3 %collective-permute-start.19 = (bf16[64,1024]{1,0:T(8,128)(2,1)S(1)}, bf16[64,1024]{1,0:T(8,128)(2,1)S(1)}, u32[]{:S(2)}, u32[]{:S(2)}) collective-permute-start(bf16[64,1024]{1,0:T(8,128)(2,1)S(1)} %get-tuple-element.145), channel_id=1, source_target_pairs={{0,48},{8,56},{16,32},{24,40},{32,80},{40,88},{48,64},{56,72},{64,... | collective-permute-start | bytes 393224 | tf_op jit(solution)/shard_map/ppermute | solution.py:643
  59.2 8.2 %collective-permute-start.20 = (bf16[64,1024]{1,0:T(8,128)(2,1)S(1)}, bf16[64,1024]{1,0:T(8,128)(2,1)S(1)}, u32[]{:S(2)}, u32[]{:S(2)}) collective-permute-start(bf16[64,1024]{1,0:T(8,128)(2,1)S(1)} %get-tuple-element.146), channel_id=1, source_target_pairs={{0,32},{8,40},{16,48},{24,56},{32,64},{40,72},{48,80},{56,88},{64,... | collective-permute-start | bytes 393224 | tf_op jit(solution)/shard_map/ppermute | solution.py:643
  61.4 8.3 %collective-permute-start.21 = (bf16[64,1024]{1,0:T(8,128)(2,1)S(1)}, bf16[64,1024]{1,0:T(8,128)(2,1)S(1)}, u32[]{:S(2)}, u32[]{:S(2)}) collective-permute-start(bf16[64,1024]{1,0:T(8,128)(2,1)S(1)} %get-tuple-element.150), channel_id=1, source_target_pairs={{0,224},{8,232},{16,240},{24,248},{32,0},{40,8},{48,16},{56,24},{6... | collective-permute-start | bytes 393224 | tf_op jit(solution)/shard_map/ppermute | solution.py:643
  64.4 7.5 %collective-permute-start.22 = (bf16[64,1024]{1,0:T(8,128)(2,1)S(1)}, bf16[64,1024]{1,0:T(8,128)(2,1)S(1)}, u32[]{:S(2)}, u32[]{:S(2)}) collective-permute-start(bf16[64,1024]{1,0:T(8,128)(2,1)S(1)} %get-tuple-element.151), channel_id=1, source_target_pairs={{0,240},{8,248},{16,224},{24,232},{32,16},{40,24},{48,0},{56,8},{6... | collective-permute-start | bytes 393224 | tf_op jit(solution)/shard_map/ppermute | solution.py:643
  67.5 6.3 %collective-permute-start.23 = (bf16[64,1024]{1,0:T(8,128)(2,1)S(1)}, bf16[64,1024]{1,0:T(8,128)(2,1)S(1)}, u32[]{:S(2)}, u32[]{:S(2)}) collective-permute-start(bf16[64,1024]{1,0:T(8,128)(2,1)S(1)} %get-tuple-element.152), channel_id=1, source_target_pairs={{0,32},{8,40},{16,48},{24,56},{32,64},{40,72},{48,80},{56,88},{64,... | collective-permute-start | bytes 393224 | tf_op jit(solution)/shard_map/ppermute | solution.py:643
  69.0 5.5 %collective-permute-start.24 = (bf16[256,256]{1,0:T(8,128)(2,1)S(1)}, bf16[256,256]{1,0:T(8,128)(2,1)S(1)}, u32[]{:S(2)}, u32[]{:S(2)}) collective-permute-start(bf16[256,256]{1,0:T(8,128)(2,1)S(1)} %get-tuple-element.155), channel_id=1, source_target_pairs={{0,4},{1,5},{2,6},{3,7},{4,0},{5,1},{6,2},{7,3},{8,12},{9,13},{10,... | collective-permute-start | bytes 393224 | tf_op jit(solution)/shard_map/ppermute | solution.py:748
  (8 other events, 16.0 us)
where the time goes:
time: 76.5 us; the launch traced here: 75.2 us
  starting transfers between devices  42.8 us (56%)
  waiting for transfers between devices  15.2 us (20%)
  Pallas kernels  14.9 us (19%)
  local copies, waits for them, and re-layouts  1.44 us (2%)
  between operations  0.93 us (1%)
    ppermute x11, starting transfers between devices, swap(): return lax.ppermute(array, 'ctx', [(i, i ^ bit) for i in range(32)])  16.8 us
    ppermute x9, starting transfers between devices, turn_z(): lax.ppermute(array, 'ctx', [(i, (i // 4 + step) % 8 * 4 + (i % 4 ^ side))...  15.4 us
    pallas_call x22, Pallas kernels, __call__(): pl.pallas_call(body, out_shape=tuple(shapes), in_specs=specs, out_specs=t...  14.9 us
    ppermute x9, waiting for transfers between devices, turn_z(): lax.ppermute(array, 'ctx', [(i, (i // 4 + step) % 8 * 4 + (i % 4 ^ side))...  6.17 us
    ppermute x1, starting transfers between devices, chain(): return lax.ppermute(array, 'ctx', pairs + [(b, a) for a, b in pairs])  5.06 us
    ppermute x3, starting transfers between devices, turn_x(): return lax.ppermute(array, 'head', pairs)  4.84 us
    ppermute x11, waiting for transfers between devices, swap(): return lax.ppermute(array, 'ctx', [(i, i ^ bit) for i in range(32)])  4.48 us
    ppermute x3, waiting for transfers between devices, turn_x(): return lax.ppermute(array, 'head', pairs)  3.67 us
  transfers between devices with their start and end apart: 25, of which 11 were waited for; matrix products, arithmetic and copies ran while one was open for 0% of the time, Pallas kernels for 17%

commit v1 on v0

--- a/solution.py
+++ b/solution.py
@@ -740,7 +740,7 @@
         third_step_kernel, [half] * 4, up, parts[2], down, parts[7], placed=True, flops=1e3
     )
     up = [turn_z(up_cross, 1, 2), turn_z(up_straight, 1)]
-    from_down = [turn_z(straight, -1), turn_z(cross, -1, 2)]
+    from_down = [turn_z(cross, -1, 2), turn_z(straight, -1)]
     if head_count == 8:
         keep_x, send_x = call(
             sum_x_kernel, [((T, T), F32), ((T, T), BF)], pieces[0], *came, flops=1e3

time: 76.5 us -> 75 us (0.980); the launches traced: 75.2 us -> 74.8 us
    ppermute x9, starting transfers between devices: 15.4 us -> 14.2 us  [turn_z(): lax.ppermute(array, 'ctx', [(i, (i // 4 + step) % 8 * 4 + (i % 4 ^ side))...]
    ppermute x1, starting transfers between devices: 0.68 us -> 1.58 us  [local(): came_x = lax.ppermute(send_x, 'head', [(i, i ^ 4) for i in range(8)])]
  transfers between devices with their start and end apart: 25 -> 25, of which waited for: 11 -> 12; matrix products, arithmetic and copies ran while one was open for 0% -> 0% of each run, Pallas kernels for 17% -> 17%
where the time goes in v1:
time: 75 us; the launch traced here: 74.8 us
  starting transfers between devices  42.4 us (57%)
  waiting for transfers between devices  15.2 us (20%)
  Pallas kernels  14.9 us (20%)
  local copies, waits for them, and re-layouts  1.44 us (2%)
  between operations  0.92 us (1%)
    ppermute x11, starting transfers between devices, swap(): return lax.ppermute(array, 'ctx', [(i, i ^ bit) for i in range(32)])  16.8 us
    pallas_call x22, Pallas kernels, __call__(): pl.pallas_call(body, out_shape=tuple(shapes), in_specs=specs, out_specs=t...  14.9 us
    ppermute x9, starting transfers between devices, turn_z(): lax.ppermute(array, 'ctx', [(i, (i // 4 + step) % 8 * 4 + (i % 4 ^ side))...  14.2 us
    ppermute x9, waiting for transfers between devices, turn_z(): lax.ppermute(array, 'ctx', [(i, (i // 4 + step) % 8 * 4 + (i % 4 ^ side))...  6.43 us
    ppermute x1, starting transfers between devices, chain(): return lax.ppermute(array, 'ctx', pairs + [(b, a) for a, b in pairs])  5.06 us
    ppermute x3, starting transfers between devices, turn_x(): return lax.ppermute(array, 'head', pairs)  4.84 us
    ppermute x11, waiting for transfers between devices, swap(): return lax.ppermute(array, 'ctx', [(i, i ^ bit) for i in range(32)])  4.48 us
    ppermute x3, waiting for transfers between devices, turn_x(): return lax.ppermute(array, 'head', pairs)  3.42 us
  transfers between devices with their start and end apart: 25, of which 12 were waited for; matrix products, arithmetic and copies ran while one was open for 0% of the time, Pallas kernels for 17%

profile of v1, /device:TPU:2, one launch (start us, length us, event | category | flops | bytes accessed | tf_op | source)
XLA Modules:
  0.0 74.8 jit_solution(8979448492908738800)
XLA Ops:
  0.7 1.4 %copy-done.1 = bf16[256,2048]{1,0:T(8,128)(2,1)S(1)} copy-done((bf16[256,2048]{1,0:T(8,128)(2,1)S(1)}, bf16[256,2048]{1,0:T(8,128)(2,1)}, u32[]{:S(2)}) %copy-start.1) | copy-done | bytes 1048600
  2.4 3.2 %collective-permute-start = (bf16[16,1024]{1,0:T(8,128)(2,1)S(1)}, bf16[16,1024]{1,0:T(8,128)(2,1)S(1)}, u32[]{:S(2)}, u32[]{:S(2)}) collective-permute-start(bf16[16,1024]{1,0:T(8,128)(2,1)S(1)} %get-tuple-element.83.refs_1_), channel_id=1, source_target_pairs={{0,16},{8,24},{16,0},{24,8},{32,48},{40,56},{48,32},{56,40},{64,80... | collective-permute-start | bytes 98312 | tf_op jit(solution)/shard_map/ppermute | solution.py:636
  5.7 1.3 %shard_map.158 = (bf16[256,768]{1,0:T(8,128)(2,1)S(1)}, f32[256,768]{1,0:T(8,128)S(1)}, f32[8,128]{1,0:T(8,128)S(1)}) custom-call(f32[8,128]{1,0:T(8,128)S(1)} %get-tuple-element.81.refs_0_, bf16[256,2048]{1,0:T(8,128)(2,1)S(1)} %copy-done.1, bf16[3,2048,256]{2,1,0:T(8,128)(2,1)S(1)} %bitcast.3, bf16[256,256]{1,0:T(8,128)(2,1)S(1)} %copy-done.10), custom_call_target="tpu_custom_call" | custom-call | flops 10000000000 | bytes 1000 | tf_op jit(solution)/shard_map/pallas_call | solution.py:138
  7.0 0.9 %collective-permute-done.refs_2_.refs_1_ = bf16[16,1024]{1,0:T(8,128)(2,1)S(1)} collective-permute-done((bf16[16,1024]{1,0:T(8,128)(2,1)S(1)}, bf16[16,1024]{1,0:T(8,128)(2,1)S(1)}, u32[]{:S(2)}, u32[]{:S(2)}) %collective-permute-start) | collective-permute-done | bytes 32800 | tf_op jit(solution)/shard_map/ppermute | solution.py:636
  8.0 4.6 %collective-permute-start.3 = (bf16[16,1024]{1,0:T(8,128)(2,1)S(1)}, bf16[16,1024]{1,0:T(8,128)(2,1)S(1)}, u32[]{:S(2)}, u32[]{:S(2)}) collective-permute-start(bf16[16,1024]{1,0:T(8,128)(2,1)S(1)} %get-tuple-element.89), channel_id=1, source_target_pairs={{0,96},{8,104},{16,112},{24,120},{32,64},{40,72},{48,80},{56,88},{... | collective-permute-start | bytes 98312 | tf_op jit(solution)/shard_map/ppermute | solution.py:636
  13.3 5.1 %collective-permute-start.4 = (bf16[16,2048]{1,0:T(8,128)(2,1)S(1)}, bf16[16,2048]{1,0:T(8,128)(2,1)S(1)}, u32[]{:S(2)}, u32[]{:S(2)}) collective-permute-start(bf16[16,2048]{1,0:T(8,128)(2,1)S(1)} %get-tuple-element.90), channel_id=1, source_target_pairs={{8,16},{24,32},{40,48},{56,64},{72,80},{88,96},{104,112},{120,128}... | collective-permute-start | bytes 196616 | tf_op jit(solution)/shard_map/ppermute | solution.py:640
  18.4 1.3 %shard_map.160 = (f32[256,512]{1,0:T(8,128)S(1)}, bf16[256,1024]{1,0:T(8,128)(2,1)S(1)}, bf16[256,1024]{1,0:T(8,128)(2,1)S(1)}, f32[256,1024]{1,0:T(8,128)S(1)},...) custom-call(f32[8,128]{1,0:T(8,128)S(1)} %get-tuple-element.85.refs_0_, ...), custom_call_target="tpu_custom_call" | custom-call | flops 10000000000 | bytes 1000 | tf_op jit(solution)/shard_map/pallas_call | solution.py:138
  19.7 0.8 %collective-permute-done.4.refs_5_.refs_6_.refs_3_ = bf16[16,2048]{1,0:T(8,128)(2,1)S(1)} collective-permute-done((bf16[16,2048]{1,0:T(8,128)(2,1)S(1)}, bf16[16,2048]{1,0:T(8,128)(2,1)S(1)}, u32[]{:S(2)}, u32[]{:S(2)}) %collective-permute-start.4) | collective-permute-done | bytes 65568 | tf_op jit(solution)/shard_map/ppermute | solution.py:640
  22.3 1.5 %shard_map.163 = (bf16[256,256]{1,0:T(8,128)(2,1)S(1)}, bf16[256,384]{1,0:T(8,128)(2,1)S(1)}, bf16[16,512]{1,0:T(8,128)(2,1)S(1)}, bf16[48,512]{1,0:T(8,128)(2,1...) custom-call(f32[8,128]{1,0:T(8,128)S(1)} %get-tuple-element.93.refs_0_, bf16[3,2048,256]{2,1,0:T(8,128)(2,1)S(1)} %bitcast.4, ...), custom_call_target="tpu_custom_call" | custom-call | flops 10000000000 | bytes 1000 | tf_op jit(solution)/shard_map/pallas_call | solution.py:138
  23.8 1.3 %collective-permute-start.6 = (bf16[48,512]{1,0:T(8,128)(2,1)S(1)}, bf16[48,512]{1,0:T(8,128)(2,1)S(1)}, u32[]{:S(2)}, u32[]{:S(2)}) collective-permute-start(bf16[48,512]{1,0:T(8,128)(2,1)S(1)} %get-tuple-element.107.refs_2_), channel_id=1, source_target_pairs={{0,16},{8,24},{16,0},{24,8},{32,48},{40,56},{48,32},{56,40},{64,80... | collective-permute-start | bytes 147464 | tf_op jit(solution)/shard_map/ppermute | solution.py:636
  25.1 2.1 %shard_map.164 = (bf16[608,512]{1,0:T(8,128)(2,1)S(1)}, f32[256,512]{1,0:T(8,128)S(1)}, f32[8,128]{1,0:T(8,128)S(1)}) custom-call(f32[8,128]{1,0:T(8,128)S(1)} %get-tuple-element.97.refs_0_, bf16[256,768]{1,0:T(8,128)(2,1)S(1)} %get-tuple-element.86.refs_1_.refs_2_, f32[256,768]{1,0:T(8,128)S(1)} %get-tuple-element.87.refs_2_.refs_3_, ...), custom_call_target="tpu_custom_call" | custom-call | flops 10000000000 | bytes 1000 | tf_op jit(solution)/shard_map/pallas_call | solution.py:138
  27.3 2.2 %collective-permute-done.6.refs_3_ = bf16[48,512]{1,0:T(8,128)(2,1)S(1)} collective-permute-done((bf16[48,512]{1,0:T(8,128)(2,1)S(1)}, bf16[48,512]{1,0:T(8,128)(2,1)S(1)}, u32[]{:S(2)}, u32[]{:S(2)}) %collective-permute-start.6) | collective-permute-done | bytes 49184 | tf_op jit(solution)/shard_map/ppermute | solution.py:636
  30.2 0.9 %collective-permute-done.7.refs_2_.refs_6_ = bf16[112,512]{1,0:T(8,128)(2,1)S(1)} collective-permute-done((bf16[112,512]{1,0:T(8,128)(2,1)S(1)}, bf16[112,512]{1,0:T(8,128)(2,1)S(1)}, u32[]{:S(2)}, u32[]{:S(2)}) %collective-permute-start.7) | collective-permute-done | bytes 114720 | tf_op jit(solution)/shard_map/ppermute | solution.py:636
  32.0 3.8 %collective-permute-start.11 = (bf16[144,1024]{1,0:T(8,128)(2,1)S(1)}, bf16[144,1024]{1,0:T(8,128)(2,1)S(1)}, u32[]{:S(2)}, u32[]{:S(2)}) collective-permute-start(bf16[144,1024]{1,0:T(8,128)(2,1)S(1)} %get-tuple-element.121), channel_id=1, source_target_pairs={{0,224},{8,232},{16,240},{24,248},{32,0},{40,8},{48,16},{56,24},{6... | collective-permute-start | bytes 884744 | tf_op jit(solution)/shard_map/ppermute | solution.py:643
  35.8 1.3 %shard_map.168 = (bf16[64,1024]{1,0:T(8,128)(2,1)S(1)}, bf16[64,1024]{1,0:T(8,128)(2,1)S(1)}, bf16[128,1024]{1,0:T(8,128)(2,1)S(1)}, bf16[128,1024]{1,0:T(8,128)(2,1)}, f32[8,128]{1,0:T(8,128)S(1)}) custom-call(f32[8,128]{1,0:T(8,128)S(1)} %get-tuple-element.116.refs_0_, bf16[1024,512]{1,0:T(8,128)(2,1)S(1)} %get-tuple-element.111.refs_3_.refs_1_, ...), custom_call_target="tpu_custom_call" | custom-call | flops 10000000000 | bytes 1000 | tf_op jit(solution)/shard_map/pallas_call | solution.py:138
  37.1 2.8 %collective-permute-start.12 = (bf16[128,1024]{1,0:T(8,128)(2,1)S(1)}, bf16[128,1024]{1,0:T(8,128)(2,1)S(1)}, u32[]{:S(2)}, u32[]{:S(2)}) collective-permute-start(bf16[128,1024]{1,0:T(8,128)(2,1)S(1)} %get-tuple-element.123), channel_id=1, source_target_pairs={{0,16},{8,24},{16,0},{24,8},{32,48},{40,56},{48,32},{56,40},{64,80... | collective-permute-start | bytes 786440 | tf_op jit(solution)/shard_map/ppermute | solution.py:636
  39.9 1.0 %shard_map.169 = (bf16[128,1024]{1,0:T(8,128)(2,1)S(1)}, bf16[128,1024]{1,0:T(8,128)(2,1)S(1)}, bf16[128,1024]{1,0:T(8,128)(2,1)S(1)}, bf16[128,1024]{1,0:T(8,128)(2,1)S(1)}, f32[8,128]{1,0:T(8,128)S(1)}) custom-call(f32[8,128]{1,0:T(8,128)S(1)} %get-tuple-element.117.refs_0_, bf16[1024,512]{1,0:T(8,128)(2,1)S(1)} %get-tuple-element.111.refs_3_.refs_1_, ...), custom_call_target="tpu_custom_call" | custom-call | flops 10000000000 | bytes 1000 | tf_op jit(solution)/shard_map/pallas_call | solution.py:138
  40.9 2.1 %collective-permute-done.10.refs_4_.refs_2_ = bf16[144,1024]{1,0:T(8,128)(2,1)S(1)} collective-permute-done((bf16[144,1024]{1,0:T(8,128)(2,1)S(1)}, bf16[144,1024]{1,0:T(8,128)(2,1)S(1)}, u32[]{:S(2)}, u32[]{:S(2)}) %collective-permute-start.10) | collective-permute-done | bytes 294944 | tf_op jit(solution)/shard_map/ppermute | solution.py:643
  43.1 3.2 %collective-permute-start.13 = (bf16[16,512]{1,0:T(8,128)(2,1)S(1)}, bf16[16,512]{1,0:T(8,128)(2,1)S(1)}, u32[]{:S(2)}, u32[]{:S(2)}) collective-permute-start(bf16[16,512]{1,0:T(8,128)(2,1)S(1)} %get-tuple-element.131), channel_id=1, source_target_pairs={{0,64},{8,72},{16,80},{24,88},{32,96},{40,104},{48,112},{56,120},{... | collective-permute-start | bytes 49160 | tf_op jit(solution)/shard_map/ppermute | solution.py:636
  46.8 2.8 %collective-permute-start.14 = (bf16[128,1024]{1,0:T(8,128)(2,1)S(1)}, bf16[128,1024]{1,0:T(8,128)(2,1)S(1)}, u32[]{:S(2)}, u32[]{:S(2)}) collective-permute-start(bf16[128,1024]{1,0:T(8,128)(2,1)S(1)} %get-tuple-element.135), channel_id=1, source_target_pairs={{0,32},{8,40},{16,48},{24,56},{32,64},{40,72},{48,80},{56,88},{64,... | collective-permute-start | bytes 786440 | tf_op jit(solution)/shard_map/ppermute | solution.py:643
  50.1 1.0 %shard_map.172 = (bf16[256,512]{1,0:T(8,128)(2,1)S(1)}, f32[8,128]{1,0:T(8,128)S(1)}) custom-call(f32[8,128]{1,0:T(8,128)S(1)} %get-tuple-element.126.refs_0_, bf16[256,768]{1,0:T(8,128)(2,1)S(1)} %get-tuple-element.86.refs_1_.refs_2_, f32[256,768]{1,0:T(8,128)S(1)} %get-tuple-element.87.refs_2_.refs_3_, f32[256,512]{1,0:T(8,128)S(1)} %get-tuple-element.127.refs_3_, ...), custom_call_target="tpu_custom_call" | custom-call | flops 10000000000 | bytes 1000 | tf_op jit(solution)/shard_map/pallas_call | solution.py:138
  51.1 1.0 %shard_map.173 = (bf16[512,256]{1,0:T(8,128)(2,1)S(1)}, bf16[512,256]{1,0:T(8,128)(2,1)S(1)}, bf16[512,256]{1,0:T(8,128)(2,1)S(1)}, bf16[512,256]{1,0:T(8,128)(2,1)S(1)}, f32[8,128]{1,0:T(8,128)S(1)}) custom-call(f32[8,128]{1,0:T(8,128)S(1)} %get-tuple-element.132.refs_0_, bf16[608,512]{1,0:T(8,128)(2,1)S(1)} %get-tuple-element.113.refs_5_.refs_3_.refs_1_, ...), custom_call_target="tpu_custom_call" | custom-call | flops 10000000000 | bytes 1000 | tf_op jit(solution)/shard_map/pallas_call | solution.py:138
  52.1 1.6 %collective-permute-start.16 = (bf16[512,256]{1,0:T(8,128)(2,1)S(1)}, bf16[512,256]{1,0:T(8,128)(2,1)S(1)}, u32[]{:S(2)}, u32[]{:S(2)}) collective-permute-start(bf16[512,256]{1,0:T(8,128)(2,1)S(1)} %get-tuple-element.141), channel_id=1, source_target_pairs={{0,1},{1,2},{2,3},{3,0},{4,5},{5,6},{6,7},{7,4},{8,9},{9,10},{10,1... | collective-permute-start | bytes 786440 | tf_op jit(solution)/shard_map/ppermute | solution.py:736
  53.7 1.1 %collective-permute-start.17 = (bf16[512,256]{1,0:T(8,128)(2,1)S(1)}, bf16[512,256]{1,0:T(8,128)(2,1)S(1)}, u32[]{:S(2)}, u32[]{:S(2)}) collective-permute-start(bf16[512,256]{1,0:T(8,128)(2,1)S(1)} %get-tuple-element.142), channel_id=1, source_target_pairs={{0,2},{1,3},{2,0},{3,1},{4,6},{5,7},{6,4},{7,5},{8,10},{9,11},{10,... | collective-permute-start | bytes 786440 | tf_op jit(solution)/shard_map/ppermute | solution.py:736
  54.8 2.2 %collective-permute-start.18 = (bf16[512,256]{1,0:T(8,128)(2,1)S(1)}, bf16[512,256]{1,0:T(8,128)(2,1)S(1)}, u32[]{:S(2)}, u32[]{:S(2)}) collective-permute-start(bf16[512,256]{1,0:T(8,128)(2,1)S(1)} %get-tuple-element.143), channel_id=1, source_target_pairs={{0,3},{1,0},{2,1},{3,2},{4,7},{5,4},{6,5},{7,6},{8,11},{9,8},{10,9... | collective-permute-start | bytes 786440 | tf_op jit(solution)/shard_map/ppermute | solution.py:736
  57.1 2.1 %collective-permute-start.19 = (bf16[64,1024]{1,0:T(8,128)(2,1)S(1)}, bf16[64,1024]{1,0:T(8,128)(2,1)S(1)}, u32[]{:S(2)}, u32[]{:S(2)}) collective-permute-start(bf16[64,1024]{1,0:T(8,128)(2,1)S(1)} %get-tuple-element.145), channel_id=1, source_target_pairs={{0,48},{8,56},{16,32},{24,40},{32,80},{40,88},{48,64},{56,72},{64,... | collective-permute-start | bytes 393224 | tf_op jit(solution)/shard_map/ppermute | solution.py:643
  59.4 2.0 %collective-permute-done.16.refs_2_ = bf16[512,256]{1,0:T(8,128)(2,1)S(1)} collective-permute-done((bf16[512,256]{1,0:T(8,128)(2,1)S(1)}, bf16[512,256]{1,0:T(8,128)(2,1)S(1)}, u32[]{:S(2)}, u32[]{:S(2)}) %collective-permute-start.16) | collective-permute-done | bytes 262176 | tf_op jit(solution)/shard_map/ppermute | solution.py:736
  61.4 3.0 %collective-permute-start.21 = (bf16[64,1024]{1,0:T(8,128)(2,1)S(1)}, bf16[64,1024]{1,0:T(8,128)(2,1)S(1)}, u32[]{:S(2)}, u32[]{:S(2)}) collective-permute-start(bf16[64,1024]{1,0:T(8,128)(2,1)S(1)} %get-tuple-element.150), channel_id=1, source_target_pairs={{0,240},{8,248},{16,224},{24,232},{32,16},{40,24},{48,0},{56,8},{6... | collective-permute-start | bytes 393224 | tf_op jit(solution)/shard_map/ppermute | solution.py:643
  64.9 1.4 %collective-permute-done.18.refs_4_ = bf16[512,256]{1,0:T(8,128)(2,1)S(1)} collective-permute-done((bf16[512,256]{1,0:T(8,128)(2,1)S(1)}, bf16[512,256]{1,0:T(8,128)(2,1)S(1)}, u32[]{:S(2)}, u32[]{:S(2)}) %collective-permute-start.18) | collective-permute-done | bytes 262176 | tf_op jit(solution)/shard_map/ppermute | solution.py:736
  67.1 0.9 %collective-permute-start.23 = (bf16[64,1024]{1,0:T(8,128)(2,1)S(1)}, bf16[64,1024]{1,0:T(8,128)(2,1)S(1)}, u32[]{:S(2)}, u32[]{:S(2)}) collective-permute-start(bf16[64,1024]{1,0:T(8,128)(2,1)S(1)} %get-tuple-element.152), channel_id=1, source_target_pairs={{0,32},{8,40},{16,48},{24,56},{32,64},{40,72},{48,80},{56,88},{64,... | collective-permute-start | bytes 393224 | tf_op jit(solution)/shard_map/ppermute | solution.py:643
  68.0 1.6 %collective-permute-start.24 = (bf16[256,256]{1,0:T(8,128)(2,1)S(1)}, bf16[256,256]{1,0:T(8,128)(2,1)S(1)}, u32[]{:S(2)}, u32[]{:S(2)}) collective-permute-start(bf16[256,256]{1,0:T(8,128)(2,1)S(1)} %get-tuple-element.155), channel_id=1, source_target_pairs={{0,4},{1,5},{2,6},{3,7},{4,0},{5,1},{6,2},{7,3},{8,12},{9,13},{10,... | collective-permute-start | bytes 393224 | tf_op jit(solution)/shard_map/ppermute | solution.py:748
  70.1 3.3 %collective-permute-done.23.refs_5_ = bf16[64,1024]{1,0:T(8,128)(2,1)S(1)} collective-permute-done((bf16[64,1024]{1,0:T(8,128)(2,1)S(1)}, bf16[64,1024]{1,0:T(8,128)(2,1)S(1)}, u32[]{:S(2)}, u32[]{:S(2)}) %collective-permute-start.23) | collective-permute-done | bytes 131104 | tf_op jit(solution)/shard_map/ppermute | solution.py:643
  (70 shorter events, 9.2 us)
Async XLA Ops:
  0.6 5.0 %copy-start = (bf16[2048,3,256]{2,0,1:T(8,128)(2,1)S(1)}, bf16[2048,3,256]{2,0,1:T(8,128)(2,1)}, u32[]{:S(2)}) copy-start(bf16[2048,3,256]{2,0,1:T(8,128)(2,1)} %param.15) | copy-start | bytes 9437188
  2.0 3.6 %copy-start.10 = (bf16[256,256]{1,0:T(8,128)(2,1)S(1)}, bf16[256,256]{1,0:T(8,128)(2,1)}, u32[]{:S(2)}) copy-start(bf16[256,256]{1,0:T(8,128)(2,1)} %constant.22.clone.refs_3_) | copy-start | bytes 393220
  2.4 5.5 %collective-permute-start = (bf16[16,1024]{1,0:T(8,128)(2,1)S(1)}, bf16[16,1024]{1,0:T(8,128)(2,1)S(1)}, u32[]{:S(2)}, u32[]{:S(2)}) collective-permute-start(bf16[16,1024]{1,0:T(8,128)(2,1)S(1)} %get-tuple-element.83.refs_1_), channel_id=1, source_target_pairs={{0,16},{8,24},{16,0},{24,8},{32,48},{40,56},{48,32},{56,40},{64,80... | collective-permute-start | bytes 98312 | tf_op jit(solution)/shard_map/ppermute | solution.py:636
  5.6 12.7 %copy-start.5 = (f32[256,256]{1,0:T(8,128)S(1)}, f32[256,256]{1,0:T(8,128)}, u32[]{:S(2)}) copy-start(f32[256,256]{1,0:T(8,128)} %constant.25.clone.refs_4_) | copy-start | bytes 786436
  5.6 12.7 %copy-start.6 = (f32[256,256]{1,0:T(8,128)S(1)}, f32[256,256]{1,0:T(8,128)}, u32[]{:S(2)}) copy-start(f32[256,256]{1,0:T(8,128)} %constant.24.clone.refs_3_) | copy-start | bytes 786436
  5.6 12.7 %copy-start.9 = (bf16[256,256]{1,0:T(8,128)(2,1)S(1)}, bf16[256,256]{1,0:T(8,128)(2,1)}, u32[]{:S(2)}) copy-start(bf16[256,256]{1,0:T(8,128)(2,1)} %constant.20.clone.refs_5_) | copy-start | bytes 393220
  8.0 11.7 %collective-permute-start.3 = (bf16[16,1024]{1,0:T(8,128)(2,1)S(1)}, bf16[16,1024]{1,0:T(8,128)(2,1)S(1)}, u32[]{:S(2)}, u32[]{:S(2)}) collective-permute-start(bf16[16,1024]{1,0:T(8,128)(2,1)S(1)} %get-tuple-element.89), channel_id=1, source_target_pairs={{0,96},{8,104},{16,112},{24,120},{32,64},{40,72},{48,80},{56,88},{... | collective-permute-start | bytes 98312 | tf_op jit(solution)/shard_map/ppermute | solution.py:636
  12.6 7.1 %collective-permute-start.2 = (bf16[16,1024]{1,0:T(8,128)(2,1)S(1)}, bf16[16,1024]{1,0:T(8,128)(2,1)S(1)}, u32[]{:S(2)}, u32[]{:S(2)}) collective-permute-start(bf16[16,1024]{1,0:T(8,128)(2,1)S(1)} %get-tuple-element.89), channel_id=1, source_target_pairs={{0,64},{8,72},{16,80},{24,88},{32,96},{40,104},{48,112},{56,120},{... | collective-permute-start | bytes 98312 | tf_op jit(solution)/shard_map/ppermute | solution.py:636
  12.6 7.1 %collective-permute-start.1 = (bf16[16,1024]{1,0:T(8,128)(2,1)S(1)}, bf16[16,1024]{1,0:T(8,128)(2,1)S(1)}, u32[]{:S(2)}, u32[]{:S(2)}) collective-permute-start(bf16[16,1024]{1,0:T(8,128)(2,1)S(1)} %get-tuple-element.89), channel_id=1, source_target_pairs={{0,32},{8,40},{16,48},{24,56},{32,0},{40,8},{48,16},{56,24},{64,96... | collective-permute-start | bytes 98312 | tf_op jit(solution)/shard_map/ppermute | solution.py:636
  13.3 7.3 %collective-permute-start.4 = (bf16[16,2048]{1,0:T(8,128)(2,1)S(1)}, bf16[16,2048]{1,0:T(8,128)(2,1)S(1)}, u32[]{:S(2)}, u32[]{:S(2)}) collective-permute-start(bf16[16,2048]{1,0:T(8,128)(2,1)S(1)} %get-tuple-element.90), channel_id=1, source_target_pairs={{8,16},{24,32},{40,48},{56,64},{72,80},{88,96},{104,112},{120,128}... | collective-permute-start | bytes 196616 | tf_op jit(solution)/shard_map/ppermute | solution.py:640
  20.7 1.6 %collective-permute-start.5 = (bf16[144,1024]{1,0:T(8,128)(2,1)S(1)}, bf16[144,1024]{1,0:T(8,128)(2,1)S(1)}, u32[]{:S(2)}, u32[]{:S(2)}) collective-permute-start(bf16[144,1024]{1,0:T(8,128)(2,1)S(1)} %get-tuple-element.96.refs_7_.refs_4_), channel_id=1, source_target_pairs={{0,8},{8,0},{16,24},{24,16},{32,40},{40,32},{48,56},{56,48},{64,72... | collective-permute-start | bytes 884744 | tf_op jit(solution)/shard_map/ppermute | solution.py:636
  21.4 9.6 %collective-permute-start.8 = (bf16[1024,512]{1,0:T(8,128)(2,1)S(1)}, bf16[1024,512]{1,0:T(8,128)(2,1)S(1)}, u32[]{:S(2)}, u32[]{:S(2)}) collective-permute-start(bf16[1024,512]{1,0:T(8,128)(2,1)S(1)} %get-tuple-element.112), channel_id=1, source_target_pairs={{0,8},{8,0},{16,24},{24,16},{32,40},{40,32},{48,56},{56,48},{64,72... | collective-permute-start | bytes 3145736 | tf_op jit(solution)/shard_map/ppermute | solution.py:636
  23.8 5.6 %collective-permute-start.6 = (bf16[48,512]{1,0:T(8,128)(2,1)S(1)}, bf16[48,512]{1,0:T(8,128)(2,1)S(1)}, u32[]{:S(2)}, u32[]{:S(2)}) collective-permute-start(bf16[48,512]{1,0:T(8,128)(2,1)S(1)} %get-tuple-element.107.refs_2_), channel_id=1, source_target_pairs={{0,16},{8,24},{16,0},{24,8},{32,48},{40,56},{48,32},{56,40},{64,80... | collective-permute-start | bytes 147464 | tf_op jit(solution)/shard_map/ppermute | solution.py:636
  27.2 3.9 %collective-permute-start.9 = (bf16[608,512]{1,0:T(8,128)(2,1)S(1)}, bf16[608,512]{1,0:T(8,128)(2,1)S(1)}, u32[]{:S(2)}, u32[]{:S(2)}) collective-permute-start(bf16[608,512]{1,0:T(8,128)(2,1)S(1)} %get-tuple-element.113.refs_5_.refs_3_.refs_1_), channel_id=1, source_target_pairs={{0,8},{8,0},{16,24},{24,16},{32,40},{40,32},{48,56},{56,48},{64,72... | collective-permute-start | bytes 1867784 | tf_op jit(solution)/shard_map/ppermute | solution.py:636
  29.5 1.6 %collective-permute-start.7 = (bf16[112,512]{1,0:T(8,128)(2,1)S(1)}, bf16[112,512]{1,0:T(8,128)(2,1)S(1)}, u32[]{:S(2)}, u32[]{:S(2)}) collective-permute-start(bf16[112,512]{1,0:T(8,128)(2,1)S(1)} %get-tuple-element.110.refs_1_.refs_5_), channel_id=1, source_target_pairs={{0,8},{8,0},{16,24},{24,16},{32,40},{40,32},{48,56},{56,48},{64,72... | collective-permute-start | bytes 344072 | tf_op jit(solution)/shard_map/ppermute | solution.py:636
  31.7 11.3 %collective-permute-start.10 = (bf16[144,1024]{1,0:T(8,128)(2,1)S(1)}, bf16[144,1024]{1,0:T(8,128)(2,1)S(1)}, u32[]{:S(2)}, u32[]{:S(2)}) collective-permute-start(bf16[144,1024]{1,0:T(8,128)(2,1)S(1)} %get-tuple-element.120), channel_id=1, source_target_pairs={{0,32},{8,40},{16,48},{24,56},{32,64},{40,72},{48,80},{56,88},{64,... | collective-permute-start | bytes 884744 | tf_op jit(solution)/shard_map/ppermute | solution.py:643
  32.0 11.0 %collective-permute-start.11 = (bf16[144,1024]{1,0:T(8,128)(2,1)S(1)}, bf16[144,1024]{1,0:T(8,128)(2,1)S(1)}, u32[]{:S(2)}, u32[]{:S(2)}) collective-permute-start(bf16[144,1024]{1,0:T(8,128)(2,1)S(1)} %get-tuple-element.121), channel_id=1, source_target_pairs={{0,224},{8,232},{16,240},{24,248},{32,0},{40,8},{48,16},{56,24},{6... | collective-permute-start | bytes 884744 | tf_op jit(solution)/shard_map/ppermute | solution.py:643
  37.1 9.6 %collective-permute-start.12 = (bf16[128,1024]{1,0:T(8,128)(2,1)S(1)}, bf16[128,1024]{1,0:T(8,128)(2,1)S(1)}, u32[]{:S(2)}, u32[]{:S(2)}) collective-permute-start(bf16[128,1024]{1,0:T(8,128)(2,1)S(1)} %get-tuple-element.123), channel_id=1, source_target_pairs={{0,16},{8,24},{16,0},{24,8},{32,48},{40,56},{48,32},{56,40},{64,80... | collective-permute-start | bytes 786440 | tf_op jit(solution)/shard_map/ppermute | solution.py:636
  39.9 10.2 %copy-start.11 = (bf16[256,64]{1,0:T(8,128)(2,1)S(1)}, bf16[256,64]{1,0:T(8,128)(2,1)}, u32[]{:S(2)}) copy-start(bf16[256,64]{1,0:T(8,128)(2,1)} %constant.27.clone.refs_11_) | copy-start | bytes 98308
  39.9 10.2 %copy-start.13 = (f32[96,64]{1,0:T(8,128)S(1)}, f32[96,64]{1,0:T(8,128)}, u32[]{:S(2)}) copy-start(f32[96,64]{1,0:T(8,128)} %constant.29.clone.refs_10_) | copy-start | bytes 73732
  43.1 6.9 %collective-permute-start.13 = (bf16[16,512]{1,0:T(8,128)(2,1)S(1)}, bf16[16,512]{1,0:T(8,128)(2,1)S(1)}, u32[]{:S(2)}, u32[]{:S(2)}) collective-permute-start(bf16[16,512]{1,0:T(8,128)(2,1)S(1)} %get-tuple-element.131), channel_id=1, source_target_pairs={{0,64},{8,72},{16,80},{24,88},{32,96},{40,104},{48,112},{56,120},{... | collective-permute-start | bytes 49160 | tf_op jit(solution)/shard_map/ppermute | solution.py:636
  46.8 10.2 %collective-permute-start.14 = (bf16[128,1024]{1,0:T(8,128)(2,1)S(1)}, bf16[128,1024]{1,0:T(8,128)(2,1)S(1)}, u32[]{:S(2)}, u32[]{:S(2)}) collective-permute-start(bf16[128,1024]{1,0:T(8,128)(2,1)S(1)} %get-tuple-element.135), channel_id=1, source_target_pairs={{0,32},{8,40},{16,48},{24,56},{32,64},{40,72},{48,80},{56,88},{64,... | collective-permute-start | bytes 786440 | tf_op jit(solution)/shard_map/ppermute | solution.py:643
  49.5 7.4 %collective-permute-start.15 = (bf16[128,1024]{1,0:T(8,128)(2,1)S(1)}, bf16[128,1024]{1,0:T(8,128)(2,1)S(1)}, u32[]{:S(2)}, u32[]{:S(2)}) collective-permute-start(bf16[128,1024]{1,0:T(8,128)(2,1)S(1)} %get-tuple-element.137), channel_id=1, source_target_pairs={{0,224},{8,232},{16,240},{24,248},{32,0},{40,8},{48,16},{56,24},{6... | collective-permute-start | bytes 786440 | tf_op jit(solution)/shard_map/ppermute | solution.py:643
  52.1 9.3 %collective-permute-start.16 = (bf16[512,256]{1,0:T(8,128)(2,1)S(1)}, bf16[512,256]{1,0:T(8,128)(2,1)S(1)}, u32[]{:S(2)}, u32[]{:S(2)}) collective-permute-start(bf16[512,256]{1,0:T(8,128)(2,1)S(1)} %get-tuple-element.141), channel_id=1, source_target_pairs={{0,1},{1,2},{2,3},{3,0},{4,5},{5,6},{6,7},{7,4},{8,9},{9,10},{10,1... | collective-permute-start | bytes 786440 | tf_op jit(solution)/shard_map/ppermute | solution.py:736
  53.7 10.7 %collective-permute-start.17 = (bf16[512,256]{1,0:T(8,128)(2,1)S(1)}, bf16[512,256]{1,0:T(8,128)(2,1)S(1)}, u32[]{:S(2)}, u32[]{:S(2)}) collective-permute-start(bf16[512,256]{1,0:T(8,128)(2,1)S(1)} %get-tuple-element.142), channel_id=1, source_target_pairs={{0,2},{1,3},{2,0},{3,1},{4,6},{5,7},{6,4},{7,5},{8,10},{9,11},{10,... | collective-permute-start | bytes 786440 | tf_op jit(solution)/shard_map/ppermute | solution.py:736
  54.8 11.6 %collective-permute-start.18 = (bf16[512,256]{1,0:T(8,128)(2,1)S(1)}, bf16[512,256]{1,0:T(8,128)(2,1)S(1)}, u32[]{:S(2)}, u32[]{:S(2)}) collective-permute-start(bf16[512,256]{1,0:T(8,128)(2,1)S(1)} %get-tuple-element.143), channel_id=1, source_target_pairs={{0,3},{1,0},{2,1},{3,2},{4,7},{5,4},{6,5},{7,6},{8,11},{9,8},{10,9... | collective-permute-start | bytes 786440 | tf_op jit(solution)/shard_map/ppermute | solution.py:736
  57.1 9.4 %collective-permute-start.19 = (bf16[64,1024]{1,0:T(8,128)(2,1)S(1)}, bf16[64,1024]{1,0:T(8,128)(2,1)S(1)}, u32[]{:S(2)}, u32[]{:S(2)}) collective-permute-start(bf16[64,1024]{1,0:T(8,128)(2,1)S(1)} %get-tuple-element.145), channel_id=1, source_target_pairs={{0,48},{8,56},{16,32},{24,40},{32,80},{40,88},{48,64},{56,72},{64,... | collective-permute-start | bytes 393224 | tf_op jit(solution)/shard_map/ppermute | solution.py:643
  59.2 7.8 %collective-permute-start.20 = (bf16[64,1024]{1,0:T(8,128)(2,1)S(1)}, bf16[64,1024]{1,0:T(8,128)(2,1)S(1)}, u32[]{:S(2)}, u32[]{:S(2)}) collective-permute-start(bf16[64,1024]{1,0:T(8,128)(2,1)S(1)} %get-tuple-element.146), channel_id=1, source_target_pairs={{0,32},{8,40},{16,48},{24,56},{32,64},{40,72},{48,80},{56,88},{64,... | collective-permute-start | bytes 393224 | tf_op jit(solution)/shard_map/ppermute | solution.py:643
  61.4 8.2 %collective-permute-start.21 = (bf16[64,1024]{1,0:T(8,128)(2,1)S(1)}, bf16[64,1024]{1,0:T(8,128)(2,1)S(1)}, u32[]{:S(2)}, u32[]{:S(2)}) collective-permute-start(bf16[64,1024]{1,0:T(8,128)(2,1)S(1)} %get-tuple-element.150), channel_id=1, source_target_pairs={{0,240},{8,248},{16,224},{24,232},{32,16},{40,24},{48,0},{56,8},{6... | collective-permute-start | bytes 393224 | tf_op jit(solution)/shard_map/ppermute | solution.py:643
  64.4 5.7 %collective-permute-start.22 = (bf16[64,1024]{1,0:T(8,128)(2,1)S(1)}, bf16[64,1024]{1,0:T(8,128)(2,1)S(1)}, u32[]{:S(2)}, u32[]{:S(2)}) collective-permute-start(bf16[64,1024]{1,0:T(8,128)(2,1)S(1)} %get-tuple-element.151), channel_id=1, source_target_pairs={{0,224},{8,232},{16,240},{24,248},{32,0},{40,8},{48,16},{56,24},{6... | collective-permute-start | bytes 393224 | tf_op jit(solution)/shard_map/ppermute | solution.py:643
  67.1 6.3 %collective-permute-start.23 = (bf16[64,1024]{1,0:T(8,128)(2,1)S(1)}, bf16[64,1024]{1,0:T(8,128)(2,1)S(1)}, u32[]{:S(2)}, u32[]{:S(2)}) collective-permute-start(bf16[64,1024]{1,0:T(8,128)(2,1)S(1)} %get-tuple-element.152), channel_id=1, source_target_pairs={{0,32},{8,40},{16,48},{24,56},{32,64},{40,72},{48,80},{56,88},{64,... | collective-permute-start | bytes 393224 | tf_op jit(solution)/shard_map/ppermute | solution.py:643
  68.0 6.1 %collective-permute-start.24 = (bf16[256,256]{1,0:T(8,128)(2,1)S(1)}, bf16[256,256]{1,0:T(8,128)(2,1)S(1)}, u32[]{:S(2)}, u32[]{:S(2)}) collective-permute-start(bf16[256,256]{1,0:T(8,128)(2,1)S(1)} %get-tuple-element.155), channel_id=1, source_target_pairs={{0,4},{1,5},{2,6},{3,7},{4,0},{5,1},{6,2},{7,3},{8,12},{9,13},{10,... | collective-permute-start | bytes 393224 | tf_op jit(solution)/shard_map/ppermute | solution.py:748
  (8 other events, 16.0 us)

commit v2 on v1

--- a/solution.py
+++ b/solution.py
@@ -601,17 +601,17 @@
     w_out[...] = total[:, T : 2 * T]
 
 
-def grad_x_kernel(pos, y, dkv, weights, *outs):
+def grad_x_kernel(steps, pos, y, dkv, weights, *outs):
     x = pos[1] % 4
     side = pos[1] // 4
-    for step in range(4):
+    for number, step in enumerate(steps):
         for turn in range(2):
             target = (side + turn) % 2 * 4 + (x + step) % 4
             rows = pl.ds(pl.multiple_of(target * T, T), T)
             total = dot_nt(y[:T, :T], weights[0, rows, :])
             total += dot_nt(dkv[:, :T], weights[1, rows, :])
             total += dot_nt(dkv[:, T:], weights[2, rows, :])
-            outs[step][turn * T : (turn + 1) * T] = total.astype(BF)
+            outs[number][turn * T : (turn + 1) * T] = total.astype(BF)
 
 
 def sum_x_kernel(first, second, third, fourth, keep, send):
@@ -729,21 +729,28 @@
         const["met"], const["rim_mean"], placed=True,
     )
     if head_count == 8:
-        pieces = call(grad_x_kernel, [((2 * T, T), BF)] * 4, y, dkv, weights, placed=True)
+        pieces = call(
+            functools.partial(grad_x_kernel, (1, 2, 3)), [((2 * T, T), BF)] * 3,
+            y, dkv, weights, placed=True,
+        )
 
         def turn_x(array, step):
             pairs = [(i, i // 4 * 4 + (i % 4 + step) % 4) for i in range(8)]
             return lax.ppermute(array, "head", pairs)
 
-        came = [turn_x(pieces[step], step) for step in (1, 2, 3)]
+        came = [turn_x(pieces[step - 1], step) for step in (1, 2, 3)]
     up_straight, up_cross, straight, cross = call(
         third_step_kernel, [half] * 4, up, parts[2], down, parts[7], placed=True, flops=1e3
     )
     up = [turn_z(up_cross, 1, 2), turn_z(up_straight, 1)]
     from_down = [turn_z(cross, -1, 2), turn_z(straight, -1)]
     if head_count == 8:
+        (piece,) = call(
+            functools.partial(grad_x_kernel, (0,)), [((2 * T, T), BF)],
+            y, dkv, weights, placed=True, flops=1e3,
+        )
         keep_x, send_x = call(
-            sum_x_kernel, [((T, T), F32), ((T, T), BF)], pieces[0], *came, flops=1e3
+            sum_x_kernel, [((T, T), F32), ((T, T), BF)], piece, *came, flops=1e3
         )
         came_x = lax.ppermute(send_x, "head", [(i, i ^ 4) for i in range(8)])
     (last,) = call(last_step_kernel, [half], *up, keep_1, from_side, flops=1e3)

time: 75 us -> 74.8 us (level)
  waiting for transfers between devices: 15.2 us -> 14.2 us
    ppermute x3, waiting for transfers between devices: 3.42 us -> 2.42 us  [turn_x(): return lax.ppermute(array, 'head', pairs)]
    pallas_call x22 -> x23, Pallas kernels: 14.9 us -> 15.1 us  [__call__(): pl.pallas_call(body, out_shape=tuple(shapes), in_specs=specs, out_specs=t...]
  transfers between devices with their start and end apart: 25 -> 25, of which waited for: 12 -> 12; matrix products, arithmetic and copies ran while one was open for 0% -> 0% of each run, Pallas kernels for 17% -> 18%
where the time goes in v2:
time: 74.8 us; the launch traced here: 74.7 us
  starting transfers between devices  43 us (57%)
  Pallas kernels  15.1 us (20%)
  waiting for transfers between devices  14.2 us (19%)
  local copies, waits for them, and re-layouts  1.44 us (2%)
  between operations  0.93 us (1%)
    ppermute x11, starting transfers between devices, swap(): return lax.ppermute(array, 'ctx', [(i, i ^ bit) for i in range(32)])  16.8 us
    pallas_call x23, Pallas kernels, __call__(): pl.pallas_call(body, out_shape=tuple(shapes), in_specs=specs, out_specs=t...  15.1 us
    ppermute x9, starting transfers between devices, turn_z(): lax.ppermute(array, 'ctx', [(i, (i // 4 + step) % 8 * 4 + (i % 4 ^ side))...  14.8 us
    ppermute x9, waiting for transfers between devices, turn_z(): lax.ppermute(array, 'ctx', [(i, (i // 4 + step) % 8 * 4 + (i % 4 ^ side))...  6.41 us
    ppermute x1, starting transfers between devices, chain(): return lax.ppermute(array, 'ctx', pairs + [(b, a) for a, b in pairs])  5.06 us
    ppermute x3, starting transfers between devices, turn_x(): return lax.ppermute(array, 'head', pairs)  4.83 us
    ppermute x11, waiting for transfers between devices, swap(): return lax.ppermute(array, 'ctx', [(i, i ^ bit) for i in range(32)])  4.5 us
    ppermute x3, waiting for transfers between devices, turn_x(): return lax.ppermute(array, 'head', pairs)  2.42 us
  transfers between devices with their start and end apart: 25, of which 12 were waited for; matrix products, arithmetic and copies ran while one was open for 0% of the time, Pallas kernels for 18%

profile of v2, /device:TPU:2, one launch (start us, length us, event | category | flops | bytes accessed | tf_op | source)
XLA Modules:
  0.0 74.7 jit_solution(18002255603392752695)
XLA Ops:
  0.7 1.4 %copy-done.1 = bf16[256,2048]{1,0:T(8,128)(2,1)S(1)} copy-done((bf16[256,2048]{1,0:T(8,128)(2,1)S(1)}, bf16[256,2048]{1,0:T(8,128)(2,1)}, u32[]{:S(2)}) %copy-start.1) | copy-done | bytes 1048600
  2.4 3.2 %collective-permute-start = (bf16[16,1024]{1,0:T(8,128)(2,1)S(1)}, bf16[16,1024]{1,0:T(8,128)(2,1)S(1)}, u32[]{:S(2)}, u32[]{:S(2)}) collective-permute-start(bf16[16,1024]{1,0:T(8,128)(2,1)S(1)} %get-tuple-element.84.refs_1_), channel_id=1, source_target_pairs={{0,16},{8,24},{16,0},{24,8},{32,48},{40,56},{48,32},{56,40},{64,80... | collective-permute-start | bytes 98312 | tf_op jit(solution)/shard_map/ppermute | solution.py:636
  5.7 1.3 %shard_map.158 = (bf16[256,768]{1,0:T(8,128)(2,1)S(1)}, f32[256,768]{1,0:T(8,128)S(1)}, f32[8,128]{1,0:T(8,128)S(1)}) custom-call(f32[8,128]{1,0:T(8,128)S(1)} %get-tuple-element.82.refs_0_, bf16[256,2048]{1,0:T(8,128)(2,1)S(1)} %copy-done.1, bf16[3,2048,256]{2,1,0:T(8,128)(2,1)S(1)} %bitcast.3, bf16[256,256]{1,0:T(8,128)(2,1)S(1)} %copy-done.10), custom_call_target="tpu_custom_call" | custom-call | flops 10000000000 | bytes 1000 | tf_op jit(solution)/shard_map/pallas_call | solution.py:138
  7.0 0.9 %collective-permute-done.refs_2_.refs_1_ = bf16[16,1024]{1,0:T(8,128)(2,1)S(1)} collective-permute-done((bf16[16,1024]{1,0:T(8,128)(2,1)S(1)}, bf16[16,1024]{1,0:T(8,128)(2,1)S(1)}, u32[]{:S(2)}, u32[]{:S(2)}) %collective-permute-start) | collective-permute-done | bytes 32800 | tf_op jit(solution)/shard_map/ppermute | solution.py:636
  8.0 4.6 %collective-permute-start.3 = (bf16[16,1024]{1,0:T(8,128)(2,1)S(1)}, bf16[16,1024]{1,0:T(8,128)(2,1)S(1)}, u32[]{:S(2)}, u32[]{:S(2)}) collective-permute-start(bf16[16,1024]{1,0:T(8,128)(2,1)S(1)} %get-tuple-element.90), channel_id=1, source_target_pairs={{0,96},{8,104},{16,112},{24,120},{32,64},{40,72},{48,80},{56,88},{... | collective-permute-start | bytes 98312 | tf_op jit(solution)/shard_map/ppermute | solution.py:636
  13.3 5.1 %collective-permute-start.4 = (bf16[16,2048]{1,0:T(8,128)(2,1)S(1)}, bf16[16,2048]{1,0:T(8,128)(2,1)S(1)}, u32[]{:S(2)}, u32[]{:S(2)}) collective-permute-start(bf16[16,2048]{1,0:T(8,128)(2,1)S(1)} %get-tuple-element.91), channel_id=1, source_target_pairs={{8,16},{24,32},{40,48},{56,64},{72,80},{88,96},{104,112},{120,128}... | collective-permute-start | bytes 196616 | tf_op jit(solution)/shard_map/ppermute | solution.py:640
  18.4 1.3 %shard_map.160 = (f32[256,512]{1,0:T(8,128)S(1)}, bf16[256,1024]{1,0:T(8,128)(2,1)S(1)}, bf16[256,1024]{1,0:T(8,128)(2,1)S(1)}, f32[256,1024]{1,0:T(8,128)S(1)},...) custom-call(f32[8,128]{1,0:T(8,128)S(1)} %get-tuple-element.86.refs_0_, ...), custom_call_target="tpu_custom_call" | custom-call | flops 10000000000 | bytes 1000 | tf_op jit(solution)/shard_map/pallas_call | solution.py:138
  19.7 0.8 %collective-permute-done.4.refs_5_.refs_6_.refs_3_ = bf16[16,2048]{1,0:T(8,128)(2,1)S(1)} collective-permute-done((bf16[16,2048]{1,0:T(8,128)(2,1)S(1)}, bf16[16,2048]{1,0:T(8,128)(2,1)S(1)}, u32[]{:S(2)}, u32[]{:S(2)}) %collective-permute-start.4) | collective-permute-done | bytes 65568 | tf_op jit(solution)/shard_map/ppermute | solution.py:640
  22.3 1.5 %shard_map.163 = (bf16[256,256]{1,0:T(8,128)(2,1)S(1)}, bf16[256,384]{1,0:T(8,128)(2,1)S(1)}, bf16[16,512]{1,0:T(8,128)(2,1)S(1)}, bf16[48,512]{1,0:T(8,128)(2,1...) custom-call(f32[8,128]{1,0:T(8,128)S(1)} %get-tuple-element.94.refs_0_, bf16[3,2048,256]{2,1,0:T(8,128)(2,1)S(1)} %bitcast.4, ...), custom_call_target="tpu_custom_call" | custom-call | flops 10000000000 | bytes 1000 | tf_op jit(solution)/shard_map/pallas_call | solution.py:138
  23.8 1.3 %collective-permute-start.6 = (bf16[48,512]{1,0:T(8,128)(2,1)S(1)}, bf16[48,512]{1,0:T(8,128)(2,1)S(1)}, u32[]{:S(2)}, u32[]{:S(2)}) collective-permute-start(bf16[48,512]{1,0:T(8,128)(2,1)S(1)} %get-tuple-element.108.refs_2_), channel_id=1, source_target_pairs={{0,16},{8,24},{16,0},{24,8},{32,48},{40,56},{48,32},{56,40},{64,80... | collective-permute-start | bytes 147464 | tf_op jit(solution)/shard_map/ppermute | solution.py:636
  25.1 2.1 %shard_map.164 = (bf16[608,512]{1,0:T(8,128)(2,1)S(1)}, f32[256,512]{1,0:T(8,128)S(1)}, f32[8,128]{1,0:T(8,128)S(1)}) custom-call(f32[8,128]{1,0:T(8,128)S(1)} %get-tuple-element.98.refs_0_, bf16[256,768]{1,0:T(8,128)(2,1)S(1)} %get-tuple-element.87.refs_1_.refs_2_, f32[256,768]{1,0:T(8,128)S(1)} %get-tuple-element.88.refs_2_.refs_3_, ...), custom_call_target="tpu_custom_call" | custom-call | flops 10000000000 | bytes 1000 | tf_op jit(solution)/shard_map/pallas_call | solution.py:138
  27.3 2.2 %collective-permute-done.6.refs_3_ = bf16[48,512]{1,0:T(8,128)(2,1)S(1)} collective-permute-done((bf16[48,512]{1,0:T(8,128)(2,1)S(1)}, bf16[48,512]{1,0:T(8,128)(2,1)S(1)}, u32[]{:S(2)}, u32[]{:S(2)}) %collective-permute-start.6) | collective-permute-done | bytes 49184 | tf_op jit(solution)/shard_map/ppermute | solution.py:636
  30.2 0.9 %collective-permute-done.7.refs_2_.refs_6_ = bf16[112,512]{1,0:T(8,128)(2,1)S(1)} collective-permute-done((bf16[112,512]{1,0:T(8,128)(2,1)S(1)}, bf16[112,512]{1,0:T(8,128)(2,1)S(1)}, u32[]{:S(2)}, u32[]{:S(2)}) %collective-permute-start.7) | collective-permute-done | bytes 114720 | tf_op jit(solution)/shard_map/ppermute | solution.py:636
  32.0 3.8 %collective-permute-start.11 = (bf16[144,1024]{1,0:T(8,128)(2,1)S(1)}, bf16[144,1024]{1,0:T(8,128)(2,1)S(1)}, u32[]{:S(2)}, u32[]{:S(2)}) collective-permute-start(bf16[144,1024]{1,0:T(8,128)(2,1)S(1)} %get-tuple-element.122), channel_id=1, source_target_pairs={{0,224},{8,232},{16,240},{24,248},{32,0},{40,8},{48,16},{56,24},{6... | collective-permute-start | bytes 884744 | tf_op jit(solution)/shard_map/ppermute | solution.py:643
  35.8 1.3 %shard_map.168 = (bf16[64,1024]{1,0:T(8,128)(2,1)S(1)}, bf16[64,1024]{1,0:T(8,128)(2,1)S(1)}, bf16[128,1024]{1,0:T(8,128)(2,1)S(1)}, bf16[128,1024]{1,0:T(8,128)(2,1)}, f32[8,128]{1,0:T(8,128)S(1)}) custom-call(f32[8,128]{1,0:T(8,128)S(1)} %get-tuple-element.117.refs_0_, bf16[1024,512]{1,0:T(8,128)(2,1)S(1)} %get-tuple-element.112.refs_3_.refs_1_, ...), custom_call_target="tpu_custom_call" | custom-call | flops 10000000000 | bytes 1000 | tf_op jit(solution)/shard_map/pallas_call | solution.py:138
  37.1 2.8 %collective-permute-start.12 = (bf16[128,1024]{1,0:T(8,128)(2,1)S(1)}, bf16[128,1024]{1,0:T(8,128)(2,1)S(1)}, u32[]{:S(2)}, u32[]{:S(2)}) collective-permute-start(bf16[128,1024]{1,0:T(8,128)(2,1)S(1)} %get-tuple-element.124), channel_id=1, source_target_pairs={{0,16},{8,24},{16,0},{24,8},{32,48},{40,56},{48,32},{56,40},{64,80... | collective-permute-start | bytes 786440 | tf_op jit(solution)/shard_map/ppermute | solution.py:636
  39.9 1.0 %shard_map.169 = (bf16[128,1024]{1,0:T(8,128)(2,1)S(1)}, bf16[128,1024]{1,0:T(8,128)(2,1)S(1)}, bf16[128,1024]{1,0:T(8,128)(2,1)S(1)}, bf16[128,1024]{1,0:T(8,128)(2,1)S(1)}, f32[8,128]{1,0:T(8,128)S(1)}) custom-call(f32[8,128]{1,0:T(8,128)S(1)} %get-tuple-element.118.refs_0_, bf16[1024,512]{1,0:T(8,128)(2,1)S(1)} %get-tuple-element.112.refs_3_.refs_1_, ...), custom_call_target="tpu_custom_call" | custom-call | flops 10000000000 | bytes 1000 | tf_op jit(solution)/shard_map/pallas_call | solution.py:138
  40.9 2.1 %collective-permute-done.10.refs_4_.refs_2_ = bf16[144,1024]{1,0:T(8,128)(2,1)S(1)} collective-permute-done((bf16[144,1024]{1,0:T(8,128)(2,1)S(1)}, bf16[144,1024]{1,0:T(8,128)(2,1)S(1)}, u32[]{:S(2)}, u32[]{:S(2)}) %collective-permute-start.10) | collective-permute-done | bytes 294944 | tf_op jit(solution)/shard_map/ppermute | solution.py:643
  43.1 3.2 %collective-permute-start.13 = (bf16[16,512]{1,0:T(8,128)(2,1)S(1)}, bf16[16,512]{1,0:T(8,128)(2,1)S(1)}, u32[]{:S(2)}, u32[]{:S(2)}) collective-permute-start(bf16[16,512]{1,0:T(8,128)(2,1)S(1)} %get-tuple-element.132), channel_id=1, source_target_pairs={{0,64},{8,72},{16,80},{24,88},{32,96},{40,104},{48,112},{56,120},{... | collective-permute-start | bytes 49160 | tf_op jit(solution)/shard_map/ppermute | solution.py:636
  46.8 2.8 %collective-permute-start.14 = (bf16[128,1024]{1,0:T(8,128)(2,1)S(1)}, bf16[128,1024]{1,0:T(8,128)(2,1)S(1)}, u32[]{:S(2)}, u32[]{:S(2)}) collective-permute-start(bf16[128,1024]{1,0:T(8,128)(2,1)S(1)} %get-tuple-element.136), channel_id=1, source_target_pairs={{0,32},{8,40},{16,48},{24,56},{32,64},{40,72},{48,80},{56,88},{64,... | collective-permute-start | bytes 786440 | tf_op jit(solution)/shard_map/ppermute | solution.py:643
  50.1 1.0 %shard_map.172 = (bf16[256,512]{1,0:T(8,128)(2,1)S(1)}, f32[8,128]{1,0:T(8,128)S(1)}) custom-call(f32[8,128]{1,0:T(8,128)S(1)} %get-tuple-element.127.refs_0_, bf16[256,768]{1,0:T(8,128)(2,1)S(1)} %get-tuple-element.87.refs_1_.refs_2_, f32[256,768]{1,0:T(8,128)S(1)} %get-tuple-element.88.refs_2_.refs_3_, f32[256,512]{1,0:T(8,128)S(1)} %get-tuple-element.128.refs_3_, ...), custom_call_target="tpu_custom_call" | custom-call | flops 10000000000 | bytes 1000 | tf_op jit(solution)/shard_map/pallas_call | solution.py:138
  51.1 0.8 %shard_map.173 = (bf16[512,256]{1,0:T(8,128)(2,1)S(1)}, bf16[512,256]{1,0:T(8,128)(2,1)S(1)}, bf16[512,256]{1,0:T(8,128)(2,1)S(1)}, f32[8,128]{1,0:T(8,128)S(1)}) custom-call(f32[8,128]{1,0:T(8,128)S(1)} %get-tuple-element.133.refs_0_, bf16[608,512]{1,0:T(8,128)(2,1)S(1)} %get-tuple-element.114.refs_5_.refs_3_.refs_1_, ...), custom_call_target="tpu_custom_call" | custom-call | flops 10000000000 | bytes 1000 | tf_op jit(solution)/shard_map/pallas_call | solution.py:138
  51.9 1.6 %collective-permute-start.16 = (bf16[512,256]{1,0:T(8,128)(2,1)S(1)}, bf16[512,256]{1,0:T(8,128)(2,1)S(1)}, u32[]{:S(2)}, u32[]{:S(2)}) collective-permute-start(bf16[512,256]{1,0:T(8,128)(2,1)S(1)} %get-tuple-element.143), channel_id=1, source_target_pairs={{0,1},{1,2},{2,3},{3,0},{4,5},{5,6},{6,7},{7,4},{8,9},{9,10},{10,1... | collective-permute-start | bytes 786440 | tf_op jit(solution)/shard_map/ppermute | solution.py:739
  53.5 1.1 %collective-permute-start.17 = (bf16[512,256]{1,0:T(8,128)(2,1)S(1)}, bf16[512,256]{1,0:T(8,128)(2,1)S(1)}, u32[]{:S(2)}, u32[]{:S(2)}) collective-permute-start(bf16[512,256]{1,0:T(8,128)(2,1)S(1)} %get-tuple-element.144), channel_id=1, source_target_pairs={{0,2},{1,3},{2,0},{3,1},{4,6},{5,7},{6,4},{7,5},{8,10},{9,11},{10,... | collective-permute-start | bytes 786440 | tf_op jit(solution)/shard_map/ppermute | solution.py:739
  54.6 2.2 %collective-permute-start.18 = (bf16[512,256]{1,0:T(8,128)(2,1)S(1)}, bf16[512,256]{1,0:T(8,128)(2,1)S(1)}, u32[]{:S(2)}, u32[]{:S(2)}) collective-permute-start(bf16[512,256]{1,0:T(8,128)(2,1)S(1)} %get-tuple-element.145), channel_id=1, source_target_pairs={{0,3},{1,0},{2,1},{3,2},{4,7},{5,4},{6,5},{7,6},{8,11},{9,8},{10,9... | collective-permute-start | bytes 786440 | tf_op jit(solution)/shard_map/ppermute | solution.py:739
  56.9 2.1 %collective-permute-start.19 = (bf16[64,1024]{1,0:T(8,128)(2,1)S(1)}, bf16[64,1024]{1,0:T(8,128)(2,1)S(1)}, u32[]{:S(2)}, u32[]{:S(2)}) collective-permute-start(bf16[64,1024]{1,0:T(8,128)(2,1)S(1)} %get-tuple-element.147), channel_id=1, source_target_pairs={{0,48},{8,56},{16,32},{24,40},{32,80},{40,88},{48,64},{56,72},{64,... | collective-permute-start | bytes 393224 | tf_op jit(solution)/shard_map/ppermute | solution.py:643
  59.9 1.4 %collective-permute-done.16.refs_2_ = bf16[512,256]{1,0:T(8,128)(2,1)S(1)} collective-permute-done((bf16[512,256]{1,0:T(8,128)(2,1)S(1)}, bf16[512,256]{1,0:T(8,128)(2,1)S(1)}, u32[]{:S(2)}, u32[]{:S(2)}) %collective-permute-start.16) | collective-permute-done | bytes 262176 | tf_op jit(solution)/shard_map/ppermute | solution.py:739
  61.2 3.4 %collective-permute-start.21 = (bf16[64,1024]{1,0:T(8,128)(2,1)S(1)}, bf16[64,1024]{1,0:T(8,128)(2,1)S(1)}, u32[]{:S(2)}, u32[]{:S(2)}) collective-permute-start(bf16[64,1024]{1,0:T(8,128)(2,1)S(1)} %get-tuple-element.152), channel_id=1, source_target_pairs={{0,240},{8,248},{16,224},{24,232},{32,16},{40,24},{48,0},{56,8},{6... | collective-permute-start | bytes 393224 | tf_op jit(solution)/shard_map/ppermute | solution.py:643
  65.2 1.0 %collective-permute-done.18.refs_4_ = bf16[512,256]{1,0:T(8,128)(2,1)S(1)} collective-permute-done((bf16[512,256]{1,0:T(8,128)(2,1)S(1)}, bf16[512,256]{1,0:T(8,128)(2,1)S(1)}, u32[]{:S(2)}, u32[]{:S(2)}) %collective-permute-start.18) | collective-permute-done | bytes 262176 | tf_op jit(solution)/shard_map/ppermute | solution.py:739
  66.9 0.9 %collective-permute-start.23 = (bf16[64,1024]{1,0:T(8,128)(2,1)S(1)}, bf16[64,1024]{1,0:T(8,128)(2,1)S(1)}, u32[]{:S(2)}, u32[]{:S(2)}) collective-permute-start(bf16[64,1024]{1,0:T(8,128)(2,1)S(1)} %get-tuple-element.154), channel_id=1, source_target_pairs={{0,32},{8,40},{16,48},{24,56},{32,64},{40,72},{48,80},{56,88},{64,... | collective-permute-start | bytes 393224 | tf_op jit(solution)/shard_map/ppermute | solution.py:643
  67.8 1.6 %collective-permute-start.24 = (bf16[256,256]{1,0:T(8,128)(2,1)S(1)}, bf16[256,256]{1,0:T(8,128)(2,1)S(1)}, u32[]{:S(2)}, u32[]{:S(2)}) collective-permute-start(bf16[256,256]{1,0:T(8,128)(2,1)S(1)} %get-tuple-element.157), channel_id=1, source_target_pairs={{0,4},{1,5},{2,6},{3,7},{4,0},{5,1},{6,2},{7,3},{8,12},{9,13},{10,... | collective-permute-start | bytes 393224 | tf_op jit(solution)/shard_map/ppermute | solution.py:755
  69.9 3.3 %collective-permute-done.23.refs_5_ = bf16[64,1024]{1,0:T(8,128)(2,1)S(1)} collective-permute-done((bf16[64,1024]{1,0:T(8,128)(2,1)S(1)}, bf16[64,1024]{1,0:T(8,128)(2,1)S(1)}, u32[]{:S(2)}, u32[]{:S(2)}) %collective-permute-start.23) | collective-permute-done | bytes 131104 | tf_op jit(solution)/shard_map/ppermute | solution.py:643
  (71 shorter events, 9.9 us)
Async XLA Ops:
  0.6 5.0 %copy-start = (bf16[2048,3,256]{2,0,1:T(8,128)(2,1)S(1)}, bf16[2048,3,256]{2,0,1:T(8,128)(2,1)}, u32[]{:S(2)}) copy-start(bf16[2048,3,256]{2,0,1:T(8,128)(2,1)} %param.15) | copy-start | bytes 9437188
  2.0 3.6 %copy-start.10 = (bf16[256,256]{1,0:T(8,128)(2,1)S(1)}, bf16[256,256]{1,0:T(8,128)(2,1)}, u32[]{:S(2)}) copy-start(bf16[256,256]{1,0:T(8,128)(2,1)} %constant.22.clone.refs_3_) | copy-start | bytes 393220
  2.4 5.5 %collective-permute-start = (bf16[16,1024]{1,0:T(8,128)(2,1)S(1)}, bf16[16,1024]{1,0:T(8,128)(2,1)S(1)}, u32[]{:S(2)}, u32[]{:S(2)}) collective-permute-start(bf16[16,1024]{1,0:T(8,128)(2,1)S(1)} %get-tuple-element.84.refs_1_), channel_id=1, source_target_pairs={{0,16},{8,24},{16,0},{24,8},{32,48},{40,56},{48,32},{56,40},{64,80... | collective-permute-start | bytes 98312 | tf_op jit(solution)/shard_map/ppermute | solution.py:636
  5.6 12.7 %copy-start.5 = (f32[256,256]{1,0:T(8,128)S(1)}, f32[256,256]{1,0:T(8,128)}, u32[]{:S(2)}) copy-start(f32[256,256]{1,0:T(8,128)} %constant.25.clone.refs_4_) | copy-start | bytes 786436
  5.6 12.7 %copy-start.6 = (f32[256,256]{1,0:T(8,128)S(1)}, f32[256,256]{1,0:T(8,128)}, u32[]{:S(2)}) copy-start(f32[256,256]{1,0:T(8,128)} %constant.24.clone.refs_3_) | copy-start | bytes 786436
  5.6 12.7 %copy-start.9 = (bf16[256,256]{1,0:T(8,128)(2,1)S(1)}, bf16[256,256]{1,0:T(8,128)(2,1)}, u32[]{:S(2)}) copy-start(bf16[256,256]{1,0:T(8,128)(2,1)} %constant.20.clone.refs_5_) | copy-start | bytes 393220
  8.0 11.7 %collective-permute-start.3 = (bf16[16,1024]{1,0:T(8,128)(2,1)S(1)}, bf16[16,1024]{1,0:T(8,128)(2,1)S(1)}, u32[]{:S(2)}, u32[]{:S(2)}) collective-permute-start(bf16[16,1024]{1,0:T(8,128)(2,1)S(1)} %get-tuple-element.90), channel_id=1, source_target_pairs={{0,96},{8,104},{16,112},{24,120},{32,64},{40,72},{48,80},{56,88},{... | collective-permute-start | bytes 98312 | tf_op jit(solution)/shard_map/ppermute | solution.py:636
  12.6 7.1 %collective-permute-start.2 = (bf16[16,1024]{1,0:T(8,128)(2,1)S(1)}, bf16[16,1024]{1,0:T(8,128)(2,1)S(1)}, u32[]{:S(2)}, u32[]{:S(2)}) collective-permute-start(bf16[16,1024]{1,0:T(8,128)(2,1)S(1)} %get-tuple-element.90), channel_id=1, source_target_pairs={{0,64},{8,72},{16,80},{24,88},{32,96},{40,104},{48,112},{56,120},{... | collective-permute-start | bytes 98312 | tf_op jit(solution)/shard_map/ppermute | solution.py:636
  12.6 7.1 %collective-permute-start.1 = (bf16[16,1024]{1,0:T(8,128)(2,1)S(1)}, bf16[16,1024]{1,0:T(8,128)(2,1)S(1)}, u32[]{:S(2)}, u32[]{:S(2)}) collective-permute-start(bf16[16,1024]{1,0:T(8,128)(2,1)S(1)} %get-tuple-element.90), channel_id=1, source_target_pairs={{0,32},{8,40},{16,48},{24,56},{32,0},{40,8},{48,16},{56,24},{64,96... | collective-permute-start | bytes 98312 | tf_op jit(solution)/shard_map/ppermute | solution.py:636
  13.3 7.3 %collective-permute-start.4 = (bf16[16,2048]{1,0:T(8,128)(2,1)S(1)}, bf16[16,2048]{1,0:T(8,128)(2,1)S(1)}, u32[]{:S(2)}, u32[]{:S(2)}) collective-permute-start(bf16[16,2048]{1,0:T(8,128)(2,1)S(1)} %get-tuple-element.91), channel_id=1, source_target_pairs={{8,16},{24,32},{40,48},{56,64},{72,80},{88,96},{104,112},{120,128}... | collective-permute-start | bytes 196616 | tf_op jit(solution)/shard_map/ppermute | solution.py:640
  20.7 1.6 %collective-permute-start.5 = (bf16[144,1024]{1,0:T(8,128)(2,1)S(1)}, bf16[144,1024]{1,0:T(8,128)(2,1)S(1)}, u32[]{:S(2)}, u32[]{:S(2)}) collective-permute-start(bf16[144,1024]{1,0:T(8,128)(2,1)S(1)} %get-tuple-element.97.refs_7_.refs_4_), channel_id=1, source_target_pairs={{0,8},{8,0},{16,24},{24,16},{32,40},{40,32},{48,56},{56,48},{64,72... | collective-permute-start | bytes 884744 | tf_op jit(solution)/shard_map/ppermute | solution.py:636
  21.4 9.6 %collective-permute-start.8 = (bf16[1024,512]{1,0:T(8,128)(2,1)S(1)}, bf16[1024,512]{1,0:T(8,128)(2,1)S(1)}, u32[]{:S(2)}, u32[]{:S(2)}) collective-permute-start(bf16[1024,512]{1,0:T(8,128)(2,1)S(1)} %get-tuple-element.113), channel_id=1, source_target_pairs={{0,8},{8,0},{16,24},{24,16},{32,40},{40,32},{48,56},{56,48},{64,72... | collective-permute-start | bytes 3145736 | tf_op jit(solution)/shard_map/ppermute | solution.py:636
  23.8 5.6 %collective-permute-start.6 = (bf16[48,512]{1,0:T(8,128)(2,1)S(1)}, bf16[48,512]{1,0:T(8,128)(2,1)S(1)}, u32[]{:S(2)}, u32[]{:S(2)}) collective-permute-start(bf16[48,512]{1,0:T(8,128)(2,1)S(1)} %get-tuple-element.108.refs_2_), channel_id=1, source_target_pairs={{0,16},{8,24},{16,0},{24,8},{32,48},{40,56},{48,32},{56,40},{64,80... | collective-permute-start | bytes 147464 | tf_op jit(solution)/shard_map/ppermute | solution.py:636
  27.2 3.9 %collective-permute-start.9 = (bf16[608,512]{1,0:T(8,128)(2,1)S(1)}, bf16[608,512]{1,0:T(8,128)(2,1)S(1)}, u32[]{:S(2)}, u32[]{:S(2)}) collective-permute-start(bf16[608,512]{1,0:T(8,128)(2,1)S(1)} %get-tuple-element.114.refs_5_.refs_3_.refs_1_), channel_id=1, source_target_pairs={{0,8},{8,0},{16,24},{24,16},{32,40},{40,32},{48,56},{56,48},{64,72... | collective-permute-start | bytes 1867784 | tf_op jit(solution)/shard_map/ppermute | solution.py:636
  29.5 1.6 %collective-permute-start.7 = (bf16[112,512]{1,0:T(8,128)(2,1)S(1)}, bf16[112,512]{1,0:T(8,128)(2,1)S(1)}, u32[]{:S(2)}, u32[]{:S(2)}) collective-permute-start(bf16[112,512]{1,0:T(8,128)(2,1)S(1)} %get-tuple-element.111.refs_1_.refs_5_), channel_id=1, source_target_pairs={{0,8},{8,0},{16,24},{24,16},{32,40},{40,32},{48,56},{56,48},{64,72... | collective-permute-start | bytes 344072 | tf_op jit(solution)/shard_map/ppermute | solution.py:636
  31.7 11.3 %collective-permute-start.10 = (bf16[144,1024]{1,0:T(8,128)(2,1)S(1)}, bf16[144,1024]{1,0:T(8,128)(2,1)S(1)}, u32[]{:S(2)}, u32[]{:S(2)}) collective-permute-start(bf16[144,1024]{1,0:T(8,128)(2,1)S(1)} %get-tuple-element.121), channel_id=1, source_target_pairs={{0,32},{8,40},{16,48},{24,56},{32,64},{40,72},{48,80},{56,88},{64,... | collective-permute-start | bytes 884744 | tf_op jit(solution)/shard_map/ppermute | solution.py:643
  32.0 11.0 %collective-permute-start.11 = (bf16[144,1024]{1,0:T(8,128)(2,1)S(1)}, bf16[144,1024]{1,0:T(8,128)(2,1)S(1)}, u32[]{:S(2)}, u32[]{:S(2)}) collective-permute-start(bf16[144,1024]{1,0:T(8,128)(2,1)S(1)} %get-tuple-element.122), channel_id=1, source_target_pairs={{0,224},{8,232},{16,240},{24,248},{32,0},{40,8},{48,16},{56,24},{6... | collective-permute-start | bytes 884744 | tf_op jit(solution)/shard_map/ppermute | solution.py:643
  37.1 9.6 %collective-permute-start.12 = (bf16[128,1024]{1,0:T(8,128)(2,1)S(1)}, bf16[128,1024]{1,0:T(8,128)(2,1)S(1)}, u32[]{:S(2)}, u32[]{:S(2)}) collective-permute-start(bf16[128,1024]{1,0:T(8,128)(2,1)S(1)} %get-tuple-element.124), channel_id=1, source_target_pairs={{0,16},{8,24},{16,0},{24,8},{32,48},{40,56},{48,32},{56,40},{64,80... | collective-permute-start | bytes 786440 | tf_op jit(solution)/shard_map/ppermute | solution.py:636
  39.9 10.2 %copy-start.11 = (bf16[256,64]{1,0:T(8,128)(2,1)S(1)}, bf16[256,64]{1,0:T(8,128)(2,1)}, u32[]{:S(2)}) copy-start(bf16[256,64]{1,0:T(8,128)(2,1)} %constant.27.clone.refs_11_) | copy-start | bytes 98308
  39.9 10.2 %copy-start.13 = (f32[96,64]{1,0:T(8,128)S(1)}, f32[96,64]{1,0:T(8,128)}, u32[]{:S(2)}) copy-start(f32[96,64]{1,0:T(8,128)} %constant.29.clone.refs_10_) | copy-start | bytes 73732
  43.1 7.0 %collective-permute-start.13 = (bf16[16,512]{1,0:T(8,128)(2,1)S(1)}, bf16[16,512]{1,0:T(8,128)(2,1)S(1)}, u32[]{:S(2)}, u32[]{:S(2)}) collective-permute-start(bf16[16,512]{1,0:T(8,128)(2,1)S(1)} %get-tuple-element.132), channel_id=1, source_target_pairs={{0,64},{8,72},{16,80},{24,88},{32,96},{40,104},{48,112},{56,120},{... | collective-permute-start | bytes 49160 | tf_op jit(solution)/shard_map/ppermute | solution.py:636
  46.8 10.0 %collective-permute-start.14 = (bf16[128,1024]{1,0:T(8,128)(2,1)S(1)}, bf16[128,1024]{1,0:T(8,128)(2,1)S(1)}, u32[]{:S(2)}, u32[]{:S(2)}) collective-permute-start(bf16[128,1024]{1,0:T(8,128)(2,1)S(1)} %get-tuple-element.136), channel_id=1, source_target_pairs={{0,32},{8,40},{16,48},{24,56},{32,64},{40,72},{48,80},{56,88},{64,... | collective-permute-start | bytes 786440 | tf_op jit(solution)/shard_map/ppermute | solution.py:643
  49.5 7.2 %collective-permute-start.15 = (bf16[128,1024]{1,0:T(8,128)(2,1)S(1)}, bf16[128,1024]{1,0:T(8,128)(2,1)S(1)}, u32[]{:S(2)}, u32[]{:S(2)}) collective-permute-start(bf16[128,1024]{1,0:T(8,128)(2,1)S(1)} %get-tuple-element.138), channel_id=1, source_target_pairs={{0,224},{8,232},{16,240},{24,248},{32,0},{40,8},{48,16},{56,24},{6... | collective-permute-start | bytes 786440 | tf_op jit(solution)/shard_map/ppermute | solution.py:643
  51.9 9.3 %collective-permute-start.16 = (bf16[512,256]{1,0:T(8,128)(2,1)S(1)}, bf16[512,256]{1,0:T(8,128)(2,1)S(1)}, u32[]{:S(2)}, u32[]{:S(2)}) collective-permute-start(bf16[512,256]{1,0:T(8,128)(2,1)S(1)} %get-tuple-element.143), channel_id=1, source_target_pairs={{0,1},{1,2},{2,3},{3,0},{4,5},{5,6},{6,7},{7,4},{8,9},{9,10},{10,1... | collective-permute-start | bytes 786440 | tf_op jit(solution)/shard_map/ppermute | solution.py:739
  53.5 11.1 %collective-permute-start.17 = (bf16[512,256]{1,0:T(8,128)(2,1)S(1)}, bf16[512,256]{1,0:T(8,128)(2,1)S(1)}, u32[]{:S(2)}, u32[]{:S(2)}) collective-permute-start(bf16[512,256]{1,0:T(8,128)(2,1)S(1)} %get-tuple-element.144), channel_id=1, source_target_pairs={{0,2},{1,3},{2,0},{3,1},{4,6},{5,7},{6,4},{7,5},{8,10},{9,11},{10,... | collective-permute-start | bytes 786440 | tf_op jit(solution)/shard_map/ppermute | solution.py:739
  54.6 11.6 %collective-permute-start.18 = (bf16[512,256]{1,0:T(8,128)(2,1)S(1)}, bf16[512,256]{1,0:T(8,128)(2,1)S(1)}, u32[]{:S(2)}, u32[]{:S(2)}) collective-permute-start(bf16[512,256]{1,0:T(8,128)(2,1)S(1)} %get-tuple-element.145), channel_id=1, source_target_pairs={{0,3},{1,0},{2,1},{3,2},{4,7},{5,4},{6,5},{7,6},{8,11},{9,8},{10,9... | collective-permute-start | bytes 786440 | tf_op jit(solution)/shard_map/ppermute | solution.py:739
  56.9 9.4 %collective-permute-start.19 = (bf16[64,1024]{1,0:T(8,128)(2,1)S(1)}, bf16[64,1024]{1,0:T(8,128)(2,1)S(1)}, u32[]{:S(2)}, u32[]{:S(2)}) collective-permute-start(bf16[64,1024]{1,0:T(8,128)(2,1)S(1)} %get-tuple-element.147), channel_id=1, source_target_pairs={{0,48},{8,56},{16,32},{24,40},{32,80},{40,88},{48,64},{56,72},{64,... | collective-permute-start | bytes 393224 | tf_op jit(solution)/shard_map/ppermute | solution.py:643
  59.0 7.9 %collective-permute-start.20 = (bf16[64,1024]{1,0:T(8,128)(2,1)S(1)}, bf16[64,1024]{1,0:T(8,128)(2,1)S(1)}, u32[]{:S(2)}, u32[]{:S(2)}) collective-permute-start(bf16[64,1024]{1,0:T(8,128)(2,1)S(1)} %get-tuple-element.148), channel_id=1, source_target_pairs={{0,32},{8,40},{16,48},{24,56},{32,64},{40,72},{48,80},{56,88},{64,... | collective-permute-start | bytes 393224 | tf_op jit(solution)/shard_map/ppermute | solution.py:643
  61.2 8.2 %collective-permute-start.21 = (bf16[64,1024]{1,0:T(8,128)(2,1)S(1)}, bf16[64,1024]{1,0:T(8,128)(2,1)S(1)}, u32[]{:S(2)}, u32[]{:S(2)}) collective-permute-start(bf16[64,1024]{1,0:T(8,128)(2,1)S(1)} %get-tuple-element.152), channel_id=1, source_target_pairs={{0,240},{8,248},{16,224},{24,232},{32,16},{40,24},{48,0},{56,8},{6... | collective-permute-start | bytes 393224 | tf_op jit(solution)/shard_map/ppermute | solution.py:643
  64.6 5.3 %collective-permute-start.22 = (bf16[64,1024]{1,0:T(8,128)(2,1)S(1)}, bf16[64,1024]{1,0:T(8,128)(2,1)S(1)}, u32[]{:S(2)}, u32[]{:S(2)}) collective-permute-start(bf16[64,1024]{1,0:T(8,128)(2,1)S(1)} %get-tuple-element.153), channel_id=1, source_target_pairs={{0,224},{8,232},{16,240},{24,248},{32,0},{40,8},{48,16},{56,24},{6... | collective-permute-start | bytes 393224 | tf_op jit(solution)/shard_map/ppermute | solution.py:643
  66.9 6.3 %collective-permute-start.23 = (bf16[64,1024]{1,0:T(8,128)(2,1)S(1)}, bf16[64,1024]{1,0:T(8,128)(2,1)S(1)}, u32[]{:S(2)}, u32[]{:S(2)}) collective-permute-start(bf16[64,1024]{1,0:T(8,128)(2,1)S(1)} %get-tuple-element.154), channel_id=1, source_target_pairs={{0,32},{8,40},{16,48},{24,56},{32,64},{40,72},{48,80},{56,88},{64,... | collective-permute-start | bytes 393224 | tf_op jit(solution)/shard_map/ppermute | solution.py:643
  67.8 6.1 %collective-permute-start.24 = (bf16[256,256]{1,0:T(8,128)(2,1)S(1)}, bf16[256,256]{1,0:T(8,128)(2,1)S(1)}, u32[]{:S(2)}, u32[]{:S(2)}) collective-permute-start(bf16[256,256]{1,0:T(8,128)(2,1)S(1)} %get-tuple-element.157), channel_id=1, source_target_pairs={{0,4},{1,5},{2,6},{3,7},{4,0},{5,1},{6,2},{7,3},{8,12},{9,13},{10,... | collective-permute-start | bytes 393224 | tf_op jit(solution)/shard_map/ppermute | solution.py:755
  (8 other events, 16.0 us)
